TPU v7x, 128 devices: a whole 4x4x4 slice. The times are simulated.
128 devices in a mesh: dp: 64 (over z, y, x_hi, core), pipe: 2 (over x_lo).
Axes of the slice: x: 4 (x_hi: 2, x_lo: 2; x = x_hi * 2 + x_lo), y: 4, z: 4, core: 2. Of those that a mesh axis runs over, the one named last changes fastest.
Arguments:
- inputs: bfloat16 [81920, 4096], P(('pipe', 'dp')), parts along dimension 0, may hold values from -6 to 6
- out_grad: bfloat16 [81920, 4608], P(('pipe', 'dp')), parts along dimension 0, may hold values from -0.078125 to 0.078125
- a_inverse: bfloat16 [8192, 4096], P(('pipe', 'dp')), parts along dimension 0, may hold values from -1 to 2, as said below
- g_inverse: bfloat16 [9216, 4608], P(('pipe', 'dp')), parts along dimension 0, may hold values from -1 to 2, as said below
- weights: float32 [9216, 4096], P(('pipe', 'dp')), parts along dimension 0, may hold values from -6 to 6
- momentum: float32 [9216, 4096], P(('pipe', 'dp')), parts along dimension 0, may hold values from -6 to 6
Outputs:
- new_weights: float32 [9216, 4096], P(('pipe', 'dp')), parts along dimension 0
- new_momentum: float32 [9216, 4096], P(('pipe', 'dp')), parts along dimension 0
There are 2 independent parts, one for each index of `pipe`. A program takes and returns all parts, laid end to end along the dimension named above; each array names one. Nothing has to cross between parts.
Inputs may be any that keep to these rules, and one draw needn't show every extreme that they name: a_inverse is symmetric and positive definite. g_inverse is symmetric and positive definite.
All inputs are finite; a program needn't handle non-finite values.
Results may differ from a plain program's by a relative error of at most 0.0037.
Values may be sent and summed in bfloat16 or wider, within the bound.
A program may use at most 320 MiB of HBM per device.

v0:
```python
import jax
import jax.numpy as jnp
from jax import lax
from jax.sharding import PartitionSpec as P


def per_device(inputs, out_grad, a_inverse, g_inverse, weights, momentum):
    columns = out_grad
    gradient = lax.psum_scatter(
        lax.dot_general(
            columns, inputs, (((0,), (0,)), ((), ())), preferred_element_type=jnp.float32
        ),
        "dp",
        scatter_dimension=0,
        tiled=True,
    )
    grad_half = gradient.astype(jnp.bfloat16)
    columns = grad_half
    right = jnp.dot(
        columns,
        lax.all_gather(a_inverse, "dp", axis=0, tiled=True),
        preferred_element_type=jnp.float32,
    ).astype(jnp.bfloat16)
    column_block = lax.all_to_all(right, "dp", split_axis=1, concat_axis=0, tiled=True)
    update_columns = jnp.dot(
        lax.all_gather(g_inverse, "dp", axis=0, tiled=True),
        column_block,
        preferred_element_type=jnp.float32,
    )
    update = lax.all_to_all(update_columns, "dp", split_axis=0, concat_axis=1, tiled=True)
    new_momentum = 0.9 * momentum + update
    new_weights = weights - 0.5 * new_momentum
    return (new_weights, new_momentum)


def solution(mesh):
    in_specs = (
        P(("pipe", "dp"), None),
        P(("pipe", "dp"), None),
        P(("pipe", "dp"), None),
        P(("pipe", "dp"), None),
        P(("pipe", "dp"), None),
        P(("pipe", "dp"), None),
    )
    out_specs = (P(("pipe", "dp"), None), P(("pipe", "dp"), None))
    return jax.shard_map(
        per_device, mesh=mesh, in_specs=in_specs, out_specs=out_specs, check_vma=False
    )
```

profile of v0, /device:TPU:0, one launch (start us, length us, event | category | flops | bytes accessed | tf_op | source)
XLA Modules:
  0.0 927.0 jit_solution(2616181701812035454)
XLA Ops:
  7.2 0.0 all-gather.3.cloned.1.call-start
  7.2 0.7 all-gather.3.cloned.1.call-update
  7.9 0.0 reduce-scatter.4.cloned.1.call-start
  7.9 40.2 %fusion.1 = f32[4608,4096]{1,0:T(8,128)} fusion(bf16[640,4608]{1,0:T(8,128)(2,1)} %param.7, bf16[640,4096]{1,0:T(8,128)(2,1)} %param.6), kind=kOutput, calls=%fused_computation.5 | convolution fusion | flops 24159191040 | bytes 86638592 | tf_op jit(solution)/shard_map/dot_general | solution.py:10
  48.2 0.0 reduce-scatter.4.cloned.1.call-update
  48.2 0.2 all-gather.5.cloned.1.call-start
  48.4 0.5 all-gather.5.cloned.1.call-update
  48.9 122.9 %all-gather.3.cloned.1.call-done = bf16[4096,4096]{1,0:T(8,128)(2,1)} async-done(((bf16[64,4096]{1,0:T(8,128)(2,1)}), bf16[4096,4096]{1,0:T(8,128)(2,1)}) %all-gather.3.cloned.1.call-update) | async-done | bytes 33554448 | tf_op jit(solution)/shard_map/all_gather | solution.py:21
  171.9 492.1 %reduce-scatter.4.cloned.1.call-done = f32[72,4096]{1,0:T(8,128)} async-done(((f32[4608,4096]{1,0:T(8,128)}), f32[72,4096]{1,0:T(8,128)}) %reduce-scatter.4.cloned.1.call-update) | async-done | bytes 1179664
  663.9 17.3 %convolution_convert_fusion = bf16[72,4096]{1,0:T(8,128)(2,1)S(1)} fusion(bf16[4096,4096]{1,0:T(8,128)(2,1)} %all-gather.3.cloned.1.call-done, f32[72,4096]{1,0:T(8,128)} %reduce-scatter.4.cloned.1.call-done), kind=kOutput, calls=%fused_computation.1 | convolution fusion | flops 2416508928 | bytes 35323904 | tf_op jit(solution)/shard_map/dot_general | solution.py:19
  681.2 0.6 copy.15
  681.8 24.5 %all_to_all.38 = bf16[72,64,64]{0,2,1:T(8,128)(2,1)S(1)} all-to-all(bf16[72,64,64]{0,2,1:T(8,128)(2,1)S(1)} %bitcast.18), channel_id=1, replica_groups=mesh['dp'=64,'pipe'=2] {'dp'}, dimensions={1} | all-to-all | bytes 1179648 | tf_op jit(solution)/shard_map/all_to_all | solution.py:24
  706.3 0.7 copy.12
  707.0 2.1 all_to_all.31
  709.1 148.2 %all-gather.5.cloned.1.call-done = bf16[4608,4608]{1,0:T(8,128)(2,1)} async-done(((bf16[72,4608]{1,0:T(8,128)(2,1)}), bf16[4608,4608]{1,0:T(8,128)(2,1)}) %all-gather.5.cloned.1.call-update) | async-done | bytes 42467344 | tf_op jit(solution)/shard_map/all_gather | solution.py:26
  857.4 18.7 %convolution_bitcast_fusion = f32[4608,64]{0,1:T(8,128)S(1)} fusion(bf16[4608,64]{0,1:T(8,128)(2,1)S(1)} %all_to_all.31, bf16[4608,4608]{1,0:T(8,128)(2,1)} %all-gather.5.cloned.1.call-done), kind=kOutput, calls=%fused_computation | convolution fusion | flops 2717908992 | bytes 44236800 | tf_op jit(solution)/shard_map/dot_general | solution.py:25
  876.1 2.1 all_to_all.32
  878.2 1.2 copy.13
  879.4 36.9 %all_to_all.39 = f32[64,72,64]{1,2,0:T(8,128)S(1)} all-to-all(f32[64,72,64]{1,2,0:T(8,128)S(1)} %copy.13), channel_id=1, replica_groups=mesh['dp'=64,'pipe'=2] {'dp'}, dimensions={0} | all-to-all | bytes 2359296 | tf_op jit(solution)/shard_map/all_to_all | solution.py:30
  916.4 0.8 copy.16
  917.2 3.3 multiply_subtract_fusion
Async XLA Ops:
  7.2 164.7 %all-gather.3.cloned.1.call-start = ((), (), s32[]{:S(2)}) async-start(), calls=%async_computation.3 | async-start | bytes 34078720 | tf_op jit(solution)/shard_map/all_gather | solution.py:21
  7.9 656.0 %reduce-scatter.4.cloned.1.call-start = ((), (), s32[]{:S(2)}) async-start(), calls=%async_computation.5 | async-start | bytes 76677120
  48.2 809.2 %all-gather.5.cloned.1.call-start = ((), (), s32[]{:S(2)}) async-start(), calls=%async_computation.4 | async-start | bytes 43130880 | tf_op jit(solution)/shard_map/all_gather | solution.py:26
Sparse Core Ops, SparseCore 0:
  11.1 160.7 all-gather.2
  178.3 485.5 reduce-scatter.3
  667.0 190.3 all-gather.4
where the time goes:
time: 928 us; the launch traced here: 927 us
  waiting for transfers between devices  764 us (82%)
  matrix products  76.2 us (8%)
  blocking collectives  61.4 us (7%)
  between operations  13.8 us (1%)
    unnamed x4, waiting for transfers between devices  493 us
    all_gather x1, waiting for transfers between devices, per_device(): lax.all_gather(g_inverse, 'dp', axis=0, tiled=True)  148 us
    all_gather x1, waiting for transfers between devices, per_device(): lax.all_gather(a_inverse, 'dp', axis=0, tiled=True)  123 us
    dot_general x1, matrix products, per_device(): lax.dot_general(columns, inputs, (((0,), (0,)), ((), ())), preferred_elem...  40.2 us
    all_to_all x1, blocking collectives, per_device(): lax.all_to_all(update_columns, 'dp', split_axis=0, concat_axis=1, tiled=T...  36.9 us
    all_to_all x1, blocking collectives, per_device(): lax.all_to_all(right, 'dp', split_axis=1, concat_axis=0, tiled=True)  24.5 us
    dot_general x1, matrix products, per_device(): jnp.dot(lax.all_gather(g_inverse, 'dp', axis=0, tiled=True), column_block...  18.7 us
  transfers between devices with their start and end apart: 3, of which 3 were waited for; matrix products, arithmetic and copies ran while one was open for 6% of the time, Pallas kernels for 0%

commit v1 on v0

v1 whole, which is shorter than its diff:
```python
import functools

import jax
import jax.numpy as jnp
from jax import lax
from jax.experimental import pallas as pl
from jax.experimental.pallas import tpu as pltpu
from jax.sharding import PartitionSpec as P

BF = jnp.bfloat16
F32 = jnp.float32
MESH = pl.DeviceIdType.MESH
NZ, NY = 4, 4
IN, OUT, TOK = 4096, 4608, 640
HALF = OUT // 2
RZ = HALF // NZ
SEG = RZ // NY
W = 256
STEPS = IN // (2 * W)
COLS = 128


def coords():
    d = lax.axis_index("dp")
    return d // 16, (d // 4) % 4, (d // 2) % 2, d % 2


def dev(z, y, x, c):
    return {"dp": ((z * 4 + y) * 2 + x) * 2 + c}


def remote(src, dst, ssem, rsem, to):
    return pltpu.make_async_remote_copy(
        src_ref=src, dst_ref=dst, send_sem=ssem, recv_sem=rsem, device_id=to, device_id_type=MESH
    )


def greet(peers):
    barrier = pltpu.get_barrier_semaphore()
    for p in peers:
        pl.semaphore_signal(barrier, inc=1, device_id=p, device_id_type=MESH)
    pl.semaphore_wait(barrier, len(peers))


def reduce_kernel(
    in_ref, og_ref, a_ref, g_ref, xg_out, ag_out, gg_out,
    ogt, ogl, ogr, inb, inr, acc, s1a, s1b, s1c, r1a, r1bc,
    sums, s2a, s2b, s2c, r2a, r2bc, tot, sx, rx, xg,
    load_sem, ld_sem, pair_s, pair_r, s1_sem, r1_sem, s2_sem, r2_sem, x_s, x_r, yg_s, yg_r, fw_s, fw_r, ag_s, ag_r, own_sem,
):
    z, y, x, c = coords()
    core = dev(z, y, x, 1 - c)
    xpeer = dev(z, y, 1 - x, c)
    zs = [dev((z + k) % 4, y, x, c) for k in (1, 2, 3)]
    ys = [dev(z, (y + k) % 4, x, c) for k in (1, 2, 3)]
    greet([core, xpeer] + zs + ys)

    other = pl.multiple_of((1 - c) * HALF, 128)
    mine = pl.multiple_of(c * HALF, 128)

    og_x = remote(og_ref.at[:, pl.ds(other, HALF)], ogr, pair_s.at[0], pair_r.at[0], core)
    og_x.start()

    def in_x(s):
        cols = pl.ds(pl.multiple_of(s * 2 * W, 2 * W), 2 * W)
        return remote(in_ref.at[:, cols], inr.at[:, cols], pair_s.at[1 + s], pair_r.at[1 + s], core)

    for s in range(STEPS):
        in_x(s).start()

    def in_load(s):
        cols = pl.ds(pl.multiple_of(s * 2 * W, 2 * W), 2 * W)
        return pltpu.make_async_copy(in_ref.at[:, cols], inb.at[s % 2], ld_sem.at[s % 2])

    in_load(0).start()

    own_a = pltpu.make_async_copy(a_ref, ag_out.at[z, c], own_sem.at[0])
    own_g = pltpu.make_async_copy(g_ref, gg_out.at[y, x], own_sem.at[1])
    own_a.start()
    own_g.start()
    a_sends = [remote(a_ref, ag_out.at[z, c], ag_s.at[k], ag_r.at[k], zs[k]) for k in range(3)]
    g_sends = [remote(g_ref, gg_out.at[y, x], ag_s.at[3 + k], ag_r.at[3 + k], ys[k]) for k in range(3)]
    a_fwd = remote(ag_out.at[:, c], ag_out.at[:, c], ag_s.at[6], ag_r.at[6], core)
    g_fwd = remote(gg_out.at[:, x], gg_out.at[:, x], ag_s.at[7], ag_r.at[7], xpeer)
    for cp in a_sends + g_sends:
        cp.start()

    part = HALF // 3
    for i in range(3):
        cp = pltpu.make_async_copy(og_ref.at[:, pl.ds(mine + i * part, part)], ogl, load_sem.at[0])
        cp.start()
        cp.wait()

        def turn(j, _, i=i):
            lanes = pl.ds(pl.multiple_of(j * 128, 128), 128)
            ogt[pl.ds(pl.multiple_of(i * part + j * 128, 128), 128), 0:TOK] = ogl[:, lanes].T
            return 0

        lax.fori_loop(0, part // 128, turn, 0)
    og_x.wait()

    def turn_r(j, _):
        lanes = pl.ds(pl.multiple_of(j * 128, 128), 128)
        ogt[pl.ds(pl.multiple_of(j * 128, 128), 128), TOK : 2 * TOK] = ogr[:, lanes].T
        return 0

    lax.fori_loop(0, HALF // 128, turn_r, 0)

    first = (z, y)
    second = (y, z)
    stride1 = (RZ, SEG)
    stride2 = (SEG, RZ)
    axis1 = (zs, ys)
    axis2 = (ys, zs)

    def near(k, d):
        return (k + 1) % 4 if d == 0 else (k + 3) % 4

    def to(axis, d):
        return axis[0] if d == 0 else axis[2]

    def rows(t, k, j):
        return pl.ds(pl.multiple_of(k * stride1[t] + j * stride2[t], 16), SEG)

    def ch(s, t):
        return 2 * s + t

    def send_a(s, t, d):
        p = s % 2
        return remote(s1a.at[t, p, d], r1a.at[ch(s, t), d], s1_sem.at[t, p, 0, d], r1_sem.at[ch(s, t), 0, d], to(axis1[t], d))

    def send_b(s, t, d):
        p = s % 2
        return remote(s1b.at[t, p, d], r1bc.at[ch(s, t), d, 1 - d], s1_sem.at[t, p, 1, d], r1_sem.at[ch(s, t), 1, d], to(axis1[t], d))

    def send_c(s, t, d):
        p = s % 2
        return remote(s1c.at[t, p, d], r1bc.at[ch(s, t), d, d], s1_sem.at[t, p, 2, d], r1_sem.at[ch(s, t), 1, d], to(axis1[t], d))

    def send_2a(s, t, d):
        p = s % 2
        return remote(s2a.at[t, p, d], r2a.at[ch(s, t), d], s2_sem.at[t, p, 0, d], r2_sem.at[ch(s, t), 0, d], to(axis2[t], d))

    def send_2b(s, t, d):
        p = s % 2
        return remote(s2b.at[t, p, d], r2bc.at[ch(s, t), d, 1 - d], s2_sem.at[t, p, 1, d], r2_sem.at[ch(s, t), 1, d], to(axis2[t], d))

    def send_2c(s, t, d):
        p = s % 2
        return remote(s2c.at[t, p, d], r2bc.at[ch(s, t), d, d], s2_sem.at[t, p, 2, d], r2_sem.at[ch(s, t), 1, d], to(axis2[t], d))

    def send_x(s, t):
        p = s % 2
        return remote(sx.at[t, p], rx.at[ch(s, t)], x_s.at[t, p], x_r.at[ch(s, t)], xpeer)

    def tile(s, t):
        return pl.ds(pl.multiple_of(ch(s, t) * W + x * COLS, COLS), COLS)

    def send_y(s, t, k):
        here = xg.at[pl.ds(pl.multiple_of(y * SEG, 16), SEG), tile(s, t)]
        return remote(here, here, yg_s.at[t, s % 2, k], yg_r.at[ch(s, t), k], ys[k])

    def send_fw(s, t):
        here = xg.at[:, tile(s, t)]
        return remote(here, here, fw_s.at[t, s % 2], fw_r.at[ch(s, t)], xpeer)

    def arrived(ref, sem):
        pltpu.make_async_copy(ref, ref, sem).wait()

    def compute(s):
        p = s % 2
        in_load(s).wait()
        in_x(s).wait()

        @pl.when(s + 1 < STEPS)
        def _():
            in_load(s + 1).start()

        for t in range(2):
            b_own = inb[p, :, t * W : (t + 1) * W]
            b_other = inr[:, pl.ds(pl.multiple_of(ch(s, t) * W, W), W)]

            def block(i, _):
                r = pl.ds(pl.multiple_of(i * RZ, 16), RZ)
                v = jnp.dot(ogt[r, 0:TOK], b_own, preferred_element_type=F32)
                v = v + jnp.dot(ogt[r, TOK : 2 * TOK], b_other, preferred_element_type=F32)
                acc[t, p, 0, r, :] = v[:, :COLS]
                acc[t, p, 1, r, :] = v[:, COLS:]
                return 0

            lax.fori_loop(0, NZ, block, 0)
            m = first[t]
            for d in range(2):
                for j in range(4):
                    s1a[t, p, d, j] = acc[t, p, d, rows(t, (m + 2) % 4, j), :].astype(BF)
                send_a(s, t, d).start()
            for d in range(2):
                for j in range(4):
                    s1b[t, p, d, j] = acc[t, p, 1 - d, rows(t, near(m, d), j), :].astype(BF)
                send_b(s, t, d).start()

    def pass_on(s):
        p = s % 2
        for t in range(2):
            for d in range(2):
                arrived(r1a.at[ch(s, t), d], r1_sem.at[ch(s, t), 0, d])
                for j in range(4):
                    v = acc[t, p, d, rows(t, near(first[t], d), j), :] + r1a[ch(s, t), d, j].astype(F32)
                    s1c[t, p, d, j] = v.astype(BF)
                send_c(s, t, d).start()

    def sum_first(s):
        p = s % 2
        for t in range(2):
            for d in range(2):
                arrived(r1bc.at[ch(s, t), d], r1_sem.at[ch(s, t), 1, d])
            for h in range(2):
                for j in range(4):
                    v = acc[t, p, h, rows(t, first[t], j), :]
                    v = v + r1bc[ch(s, t), 0, h, j].astype(F32) + r1bc[ch(s, t), 1, h, j].astype(F32)
                    sums[t, p, h, j] = v
            m = second[t]
            for d in range(2):
                s2a[t, p, d] = sums[t, p, d, (m + 2) % 4].astype(BF)
                send_2a(s, t, d).start()
            for d in range(2):
                s2b[t, p, d] = sums[t, p, 1 - d, near(m, d)].astype(BF)
                send_2b(s, t, d).start()
            for d in range(2):
                send_a(s, t, d).wait_send()
                send_b(s, t, d).wait_send()
                send_c(s, t, d).wait_send()

    def pass_on_second(s):
        p = s % 2
        for t in range(2):
            for d in range(2):
                arrived(r2a.at[ch(s, t), d], r2_sem.at[ch(s, t), 0, d])
                v = sums[t, p, d, near(second[t], d)] + r2a[ch(s, t), d].astype(F32)
                s2c[t, p, d] = v.astype(BF)
                send_2c(s, t, d).start()

    def sum_second(s):
        p = s % 2
        for t in range(2):
            for d in range(2):
                arrived(r2bc.at[ch(s, t), d], r2_sem.at[ch(s, t), 1, d])
            for h in range(2):
                v = sums[t, p, h, second[t]]
                tot[t, p, h] = v + r2bc[ch(s, t), 0, h].astype(F32) + r2bc[ch(s, t), 1, h].astype(F32)
            sx[t, p] = tot[t, p, 1 - x]
            send_x(s, t).start()
            for d in range(2):
                send_2a(s, t, d).wait_send()
                send_2b(s, t, d).wait_send()
                send_2c(s, t, d).wait_send()

    def finish(s):
        p = s % 2
        for t in range(2):
            send_x(s, t).wait()
            v = tot[t, p, x] + rx[ch(s, t)]
            xg[pl.ds(pl.multiple_of(y * SEG, 16), SEG), tile(s, t)] = v.astype(BF)
            for k in range(3):
                send_y(s, t, k).start()

    def forward(s):
        for t in range(2):
            for k in range(3):
                send_y(s, t, k).wait()
            send_fw(s, t).start()

    def complete(s):
        for t in range(2):
            send_fw(s, t).wait()

    stages = [(7, complete), (6, forward), (5, finish), (4, sum_second), (3, pass_on_second), (2, sum_first), (1, pass_on), (0, compute)]

    def step(s, _):
        for lag, stage in stages:

            @pl.when(jnp.logical_and(s >= lag, s < STEPS + lag))
            def _(lag=lag, stage=stage):
                stage(s - lag)

        @pl.when(s == 2)
        def _():
            own_a.wait()
            for cp in a_sends:
                cp.wait()
            a_fwd.start()

        @pl.when(s == 3)
        def _():
            own_g.wait()
            for cp in g_sends:
                cp.wait()
            g_fwd.start()

        return 0

    lax.fori_loop(0, STEPS + 7, step, 0)
    out = pltpu.make_async_copy(xg, xg_out, load_sem.at[0])
    out.start()
    a_fwd.wait()
    g_fwd.wait()
    out.wait()


def reduce_call(inputs, out_grad, a_inverse, g_inverse):
    anyspace = pl.BlockSpec(memory_space=pl.ANY)
    n = 2 * STEPS
    dma = pltpu.SemaphoreType.DMA
    return pl.pallas_call(
        reduce_kernel,
        out_shape=[
            jax.ShapeDtypeStruct((RZ, IN), BF),
            jax.ShapeDtypeStruct((4, 2, IN // 64, IN), BF),
            jax.ShapeDtypeStruct((4, 2, OUT // 64, OUT), BF),
        ],
        in_specs=[anyspace] * 4,
        out_specs=[anyspace] * 3,
        scratch_shapes=[
            pltpu.VMEM((HALF, 2 * TOK), BF),
            pltpu.VMEM((TOK, HALF // 3), BF),
            pltpu.VMEM((TOK, HALF), BF),
            pltpu.VMEM((2, TOK, 2 * W), BF),
            pltpu.VMEM((TOK, IN), BF),
            pltpu.VMEM((2, 2, 2, HALF, COLS), F32),
            pltpu.VMEM((2, 2, 2, 4, SEG, COLS), BF),
            pltpu.VMEM((2, 2, 2, 4, SEG, COLS), BF),
            pltpu.VMEM((2, 2, 2, 4, SEG, COLS), BF),
            pltpu.VMEM((n, 2, 4, SEG, COLS), BF),
            pltpu.VMEM((n, 2, 2, 4, SEG, COLS), BF),
            pltpu.VMEM((2, 2, 2, 4, SEG, COLS), F32),
            pltpu.VMEM((2, 2, 2, SEG, COLS), BF),
            pltpu.VMEM((2, 2, 2, SEG, COLS), BF),
            pltpu.VMEM((2, 2, 2, SEG, COLS), BF),
            pltpu.VMEM((n, 2, SEG, COLS), BF),
            pltpu.VMEM((n, 2, 2, SEG, COLS), BF),
            pltpu.VMEM((2, 2, 2, SEG, COLS), F32),
            pltpu.VMEM((2, 2, SEG, COLS), F32),
            pltpu.VMEM((n, SEG, COLS), F32),
            pltpu.VMEM((RZ, IN), BF),
            dma((1,)),
            dma((2,)),
            dma((1 + STEPS,)),
            dma((1 + STEPS,)),
            dma((2, 2, 3, 2)),
            dma((n, 2, 2)),
            dma((2, 2, 3, 2)),
            dma((n, 2, 2)),
            dma((2, 2)),
            dma((n,)),
            dma((2, 2, 3)),
            dma((n, 3)),
            dma((2, 2)),
            dma((n,)),
            dma((8,)),
            dma((8,)),
            dma((2,)),
        ],
        compiler_params=pltpu.CompilerParams(
            collective_id=0, has_side_effects=True, vmem_limit_bytes=62 * 1024 * 1024
        ),
        cost_estimate=pl.CostEstimate(flops=24_200_000_000, bytes_accessed=40_000_000, transcendentals=0),
        name="gradient_reduce",
    )(inputs, out_grad, a_inverse, g_inverse)


def update_kernel(xg, ag, gg, u_out, rg, ub, uo, z_s, z_r, c_s, c_r, u_s, u_r, out_sem):
    z, y, x, c = coords()
    core = dev(z, y, x, 1 - c)
    zs = [dev((z + k) % 4, y, x, c) for k in (1, 2, 3)]
    offs = [(k, e) for k in range(4) for e in range(2) if (k, e) != (0, 0)]
    yx = [dev(z, (y + k) % 4, (x + e) % 2, c) for k, e in offs]
    greet([core] + zs + yx)
    my_rows = pl.ds(pl.multiple_of(c * HALF + z * RZ, 16), RZ)
    core_rows = pl.ds(pl.multiple_of(c * HALF, 16), HALF)

    def send_z(q, k):
        here = rg.at[q, my_rows]
        return remote(here, here, z_s.at[q, k], z_r.at[q, k], zs[k])

    def send_core(q):
        here = rg.at[q, core_rows]
        return remote(here, here, c_s.at[q], c_r.at[q], core)

    def tile(q):
        return pl.ds(pl.multiple_of(((q * 4 + y) * 2 + x) * COLS, COLS), COLS)

    def send_u(q, i):
        k, e = offs[i]
        owner = ((y + k) % 4) * 2 + (x + e) % 2
        return remote(ub.at[q, owner], uo.at[:, tile(q)], u_s.at[q, i], u_r.at[q, i], yx[i])

    def right(q, _):
        a_rows = ag[pl.ds(pl.multiple_of(q * COLS, COLS), COLS), :]
        v = lax.dot_general(xg[...], a_rows, (((1,), (1,)), ((), ())), preferred_element_type=F32)
        rg[q, my_rows, :] = v.astype(BF)
        for k in range(3):
            send_z(q, k).start()
        return 0

    def update(q):
        send_core(q).wait()
        v = jnp.dot(gg[...], rg[q], preferred_element_type=F32)
        ub[q] = v.reshape(8, OUT // 64, COLS)
        uo[:, tile(q)] = ub[q, y * 2 + x]
        for i in range(7):
            send_u(q, i).start()

    def gather(q, _):
        @pl.when(q < 4)
        def _():
            for k in range(3):
                send_z(q, k).wait()
            send_core(q).start()

        @pl.when(q > 0)
        def _():
            update(q - 1)

        return 0

    lax.fori_loop(0, 4, right, 0)
    lax.fori_loop(0, 5, gather, 0)

    def done(q, _):
        for i in range(7):
            send_u(q, i).wait()
        return 0

    lax.fori_loop(0, 4, done, 0)
    cp = pltpu.make_async_copy(uo, u_out, out_sem.at[0])
    cp.start()
    cp.wait()


def update_call(xg, ag, gg):
    dma = pltpu.SemaphoreType.DMA
    vmem = pl.BlockSpec(memory_space=pltpu.VMEM)
    return pl.pallas_call(
        update_kernel,
        out_shape=jax.ShapeDtypeStruct((OUT // 64, IN), F32),
        in_specs=[vmem] * 3,
        out_specs=pl.BlockSpec(memory_space=pl.ANY),
        scratch_shapes=[
            pltpu.VMEM((4, OUT, COLS), BF),
            pltpu.VMEM((4, 8, OUT // 64, COLS), F32),
            pltpu.VMEM((OUT // 64, IN), F32),
            dma((4, 3)),
            dma((4, 3)),
            dma((4,)),
            dma((4,)),
            dma((4, 7)),
            dma((4, 7)),
            dma((1,)),
        ],
        compiler_params=pltpu.CompilerParams(
            collective_id=1, has_side_effects=True, vmem_limit_bytes=56 * 1024 * 1024
        ),
        cost_estimate=pl.CostEstimate(flops=5_200_000_000, bytes_accessed=16_000_000, transcendentals=0),
        name="precondition",
    )(xg, ag, gg)


def per_device(inputs, out_grad, a_inverse, g_inverse, weights, momentum):
    xg, ag, gg = reduce_call(inputs, out_grad, a_inverse, g_inverse)
    update = update_call(xg, ag.reshape(IN // 8, IN), gg.reshape(OUT // 8, OUT))
    new_momentum = 0.9 * momentum + update
    new_weights = weights - 0.5 * new_momentum
    return (new_weights, new_momentum)


def solution(mesh):
    spec = P(("pipe", "dp"), None)
    return jax.shard_map(
        per_device, mesh=mesh, in_specs=(spec,) * 6, out_specs=(spec, spec), check_vma=False
    )
```

time: 928 us -> 280 us (0.30)
  waiting for transfers between devices: 764 us -> 0 us
  Pallas kernels: 0 us -> 276 us
  matrix products: 76.2 us -> 0 us
  blocking collectives: 61.4 us -> 0 us
  between operations: 13.8 us -> 0.68 us
    unnamed x4 -> x0, waiting for transfers between devices: 493 us -> none
    pallas_call x0 -> x2, Pallas kernels: none -> 276 us  [the longest x1 224 us: reduce_call(): pl.pallas_call(reduce_kernel, out_shape=[jax.ShapeDtypeStruct((RZ, IN), B...]
    all_gather x2 -> x0, waiting for transfers between devices: 271 us -> none  [the longest x1 148 us: per_device(): lax.all_gather(g_inverse, 'dp', axis=0, tiled=True)]
    dot_general x3 -> x0, matrix products: 76.2 us -> none  [the longest x1 40.2 us: per_device(): lax.dot_general(columns, inputs, (((0,), (0,)), ((), ())), preferred_elem...]
    all_to_all x2 -> x0, blocking collectives: 61.4 us -> none  [the longest x1 36.9 us: per_device(): lax.all_to_all(update_columns, 'dp', split_axis=0, concat_axis=1, tiled=T...]
  transfers between devices with their start and end apart: 3 -> 0, of which waited for: 3 -> 0; matrix products, arithmetic and copies ran while one was open for 6% -> 0% of each run, Pallas kernels for 0% -> 0%
where the time goes in v1:
time: 280 us; the launch traced here: 279 us
  Pallas kernels  276 us (99%)
  other arithmetic  2.96 us (1%)
    pallas_call x1, Pallas kernels, reduce_call(): pl.pallas_call(reduce_kernel, out_shape=[jax.ShapeDtypeStruct((RZ, IN), B...  224 us
    pallas_call x1, Pallas kernels, update_call(): pl.pallas_call(update_kernel, out_shape=jax.ShapeDtypeStruct((OUT // 64,...  52 us

profile of v1, /device:TPU:0, one launch (start us, length us, event | category | flops | bytes accessed | tf_op | source)
XLA Modules:
  0.0 279.4 jit_solution(4812081495196858352)
XLA Ops:
  0.6 223.7 %gradient_reduce.1 = (bf16[576,4096]{1,0:T(8,128)(2,1)}, bf16[4,2,64,4096]{3,2,1,0:T(8,128)(2,1)}, bf16[4,2,72,4608]{3,2,1,0:T(8,128)(2,1)}) custom-call(bf16[640,4096]{1,0:T(8,128)(2,1)} %in_ref.1, bf16[640,4608]{1,0:T(8,128)(2,1)} %og_ref.1, bf16[64,4096]{1,0:T(8,128)(2,1)} %a_ref.1, bf16[72,4608]{1,0:T(8,128)(2,1)} %g_ref.1), custom_call_target="tpu_custom_call" | custom-call | flops 24199999488 | bytes 40000000 | tf_op jit(solution)/shard_map/gradient_reduce/pallas_call | solution.py:314
  224.4 0.0 copy-start
  224.4 0.0 copy-start.1
  224.4 52.0 %precondition.1 = f32[72,4096]{1,0:T(8,128)} custom-call(bf16[576,4096]{1,0:T(8,128)(2,1)} %get-tuple-element.5.xg, bf16[512,4096]{1,0:T(8,128)(2,1)} %bitcast.3, bf16[576,4608]{1,0:T(8,128)(2,1)} %bitcast.2), custom_call_target="tpu_custom_call" | custom-call | flops 5200000000 | bytes 16000000 | tf_op jit(solution)/shard_map/precondition/pallas_call | solution.py:443
  276.4 0.0 copy-done
  276.4 0.0 copy-done.1
  276.5 3.0 %multiply_subtract_fusion = (f32[72,4096]{1,0:T(8,128)}, f32[72,4096]{1,0:T(8,128)}) fusion(f32[72,4096]{1,0:T(8,128)S(1)} %copy-done, f32[72,4096]{1,0:T(8,128)} %precondition.1, f32[72,4096]{1,0:T(8,128)S(1)} %copy-done.1), kind=kLoop, calls=%fused_computation | loop fusion | flops 1179648 | bytes 5898240 | tf_op jit(solution)/shard_map/sub | solution.py:472
Async XLA Ops:
  224.4 52.1 %copy-start = (f32[72,4096]{1,0:T(8,128)S(1)}, f32[72,4096]{1,0:T(8,128)}, u32[]{:S(2)}) copy-start(f32[72,4096]{1,0:T(8,128)} %param.10) | copy-start | bytes 3538948
  224.4 52.1 %copy-start.1 = (f32[72,4096]{1,0:T(8,128)S(1)}, f32[72,4096]{1,0:T(8,128)}, u32[]{:S(2)}) copy-start(f32[72,4096]{1,0:T(8,128)} %param.11) | copy-start | bytes 3538948

commit v2 on v1

v2 whole, which is shorter than its diff:
```python
import functools

import jax
import jax.numpy as jnp
from jax import lax
from jax.experimental import pallas as pl
from jax.experimental.pallas import tpu as pltpu
from jax.sharding import PartitionSpec as P

BF = jnp.bfloat16
F32 = jnp.float32
MESH = pl.DeviceIdType.MESH
NZ, NY = 4, 4
IN, OUT, TOK = 4096, 4608, 640
HALF = OUT // 2
RZ = HALF // NZ
SEG = RZ // NY
W = 256
STEPS = IN // (2 * W)
COLS = 128
LAST = STEPS + 6
G_PAIR = 11
GK = OUT // 4
SLICE = 512
A_SLICES = IN // SLICE


def coords():
    d = lax.axis_index("dp")
    return d // 16, (d // 4) % 4, (d // 2) % 2, d % 2


def dev(z, y, x, c):
    return {"dp": ((z * 4 + y) * 2 + x) * 2 + c}


def remote(src, dst, ssem, rsem, to):
    return pltpu.make_async_remote_copy(
        src_ref=src, dst_ref=dst, send_sem=ssem, recv_sem=rsem, device_id=to, device_id_type=MESH
    )


def greet(peers):
    barrier = pltpu.get_barrier_semaphore()
    for p in peers:
        pl.semaphore_signal(barrier, inc=1, device_id=p, device_id_type=MESH)
    pl.semaphore_wait(barrier, len(peers))


def reduce_kernel(
    in_ref, og_ref, a_ref, g_ref, u_out, ag_hbm, gg_hbm,
    ogt, ogr, inb, inr, acc, s1a, s1b, s1c, r1a, r1bc,
    sums, s2a, s2b, s2c, r2a, r2bc, tot, sx, rx, xg,
    load_sem, ld_sem, pair_s, pair_r, s1_sem, r1_sem, s2_sem, r2_sem, x_s, x_r, yg_s, yg_r, fw_s, fw_r, ag_s, ag_r, ra_s, ra_r, gp_s, gp_r, gf_s, gf_r, own_sem,
    al_sem, gl_sem, gst, rg, uo, z_s, z_r, c_s, c_r, u_s, u_r,
):
    z, y, x, c = coords()
    core = dev(z, y, x, 1 - c)
    xpeer = dev(z, y, 1 - x, c)
    zs = [dev((z + k) % 4, y, x, c) for k in (1, 2, 3)]
    ys = [dev(z, (y + k) % 4, x, c) for k in (1, 2, 3)]
    offs = [(k, e) for k in range(4) for e in range(2) if (k, e) != (0, 0)]
    yx = [dev(z, (y + k) % 4, (x + e) % 2, c) for k, e in offs]
    greet([core, zs[0], zs[2]] + yx)
    my_rows = pl.ds(pl.multiple_of(c * HALF + z * RZ, 16), RZ)
    core_rows = pl.ds(pl.multiple_of(c * HALF, 16), HALF)

    other = pl.multiple_of((1 - c) * HALF, 128)
    mine = pl.multiple_of(c * HALF, 128)

    og_x = remote(og_ref.at[:, pl.ds(other, HALF)], ogr, pair_s.at[0], pair_r.at[0], core)
    og_x.start()

    def in_x(s):
        cols = pl.ds(pl.multiple_of(s * 2 * W, 2 * W), 2 * W)
        return remote(in_ref.at[:, cols], inr.at[:, cols], pair_s.at[1 + s], pair_r.at[1 + s], core)

    for s in range(STEPS):
        in_x(s).start()

    def in_load(s):
        cols = pl.ds(pl.multiple_of(s * 2 * W, 2 * W), 2 * W)
        return pltpu.make_async_copy(in_ref.at[:, cols], inb.at[s % 2], ld_sem.at[s % 2])


    own_a = pltpu.make_async_copy(a_ref, ag_hbm.at[z, c], own_sem.at[0])
    own_g = pltpu.make_async_copy(g_ref, gg_hbm.at[y, x], own_sem.at[1])
    own_a.start()
    own_g.start()
    a_sends = [remote(a_ref, ag_hbm.at[z, c], ag_s.at[k], ag_r.at[k], zs[2 * k]) for k in range(2)]
    g_sends = [remote(g_ref, gg_hbm.at[y, x], ag_s.at[2 + k], ag_r.at[2 + k], ys[2 * k]) for k in range(2)]
    a_fwd = remote(ag_hbm.at[:, c], ag_hbm.at[:, c], ag_s.at[4], ag_r.at[4], core)
    g_own = remote(g_ref, gg_hbm.at[y, x], ag_s.at[5], ag_r.at[5], xpeer)
    for cp in a_sends + g_sends + [g_own]:
        cp.start()

    def relay(out, sem, i, k, other_k, axis, d):
        cols = pl.ds(pl.multiple_of(i * SLICE, SLICE), SLICE)
        from_k = (k + 3) % 4 if d == 0 else (k + 1) % 4
        here = out.at[from_k, other_k, :, cols]
        return remote(here, here, sem[0].at[i], sem[1].at[i], axis[2 * d])

    def relay_a(i, d):
        return relay(ag_hbm, (ra_s, ra_r), i, z, c, zs, d)

    def g_pair(d):
        here = gg_hbm.at[y, 1 - x]
        return remote(here, here, gp_s.at[d], gp_r.at[d], ys[2 * d])

    def g_far(e, d):
        half = OUT // 2
        here = gg_hbm.at[(y + 3 - 2 * d) % 4, e, :, d * half : (d + 1) * half]
        return remote(here, here, gf_s.at[e, d], gf_r.at[e, d], ys[2 * d])

    a_loads = [
        pltpu.make_async_copy(ag_hbm.at[i // 2, i % 2], inr.at[i * 64 : (i + 1) * 64], al_sem.at[i]) for i in range(8)
    ]

    def g_load(b):
        cols = pl.ds(b * GK, GK)
        return pltpu.make_async_copy(gg_hbm.at[:, :, :, cols], gst.at[b % 2], gl_sem.at[b % 2])

    def between(s, lo, n):
        return jnp.logical_and(s >= lo, s < lo + n)

    def background(s):
        @pl.when(s == 1)
        def _():
            for cp in a_sends:
                cp.wait()

        @pl.when(s == G_PAIR)
        def _():
            g_own.wait()
            for d in range(2):
                g_pair(d).start()

        @pl.when(between(s, 1, A_SLICES // 2))
        def _():
            relay_a(2 * (s - 1), 0).start()
            relay_a(2 * (s - 1) + 1, 1).start()

        @pl.when(between(s, 3, A_SLICES // 2))
        def _():
            relay_a(2 * (s - 3), 0).wait()
            relay_a(2 * (s - 3) + 1, 1).wait()

        @pl.when(s == 3 + A_SLICES // 2)
        def _():
            own_a.wait()
            a_fwd.start()

        @pl.when(s == 5 + A_SLICES // 2)
        def _():
            a_fwd.wait()
            for cp in a_loads:
                cp.start()

    part = HALF // 6

    def og_load(i):
        return pltpu.make_async_copy(
            og_ref.at[:, pl.ds(mine + i * part, part)], inb.at[i % 2, :, 0:part], ld_sem.at[i % 2]
        )

    og_load(0).start()
    for i in range(6):
        if i < 5:
            og_load(i + 1).start()
        og_load(i).wait()
        for j in range(part // 128):
            ogt[i * part + j * 128 : i * part + (j + 1) * 128, 0:TOK] = inb[i % 2, :, j * 128 : (j + 1) * 128].T
    in_load(0).start()
    og_x.wait()

    def turn_r(j, _):
        lanes = pl.ds(pl.multiple_of(j * 128, 128), 128)
        ogt[pl.ds(pl.multiple_of(j * 128, 128), 128), TOK : 2 * TOK] = ogr[:, lanes].T
        return 0

    lax.fori_loop(0, HALF // 128, turn_r, 0)

    def kind(s, t):
        return t

    def first(s, t):
        return z + kind(s, t) * (y - z)

    def second(s, t):
        return y + kind(s, t) * (z - y)

    def to(s, t, stage, d):
        e = kind(s, t) if stage == 1 else 1 - kind(s, t)
        k = 1 if d == 0 else 3
        return dev((z + (1 - e) * k) % 4, (y + e * k) % 4, x, c)

    def near(k, d):
        return (k + 1) % 4 if d == 0 else (k + 3) % 4

    def rows(s, t, k, j):
        stride1 = RZ + kind(s, t) * (SEG - RZ)
        return pl.ds(pl.multiple_of(k * stride1 + j * (RZ + SEG - stride1), 16), SEG)

    def ch(s, t):
        return 2 * s + t

    def send_a(s, t, d):
        p = s % 2
        return remote(s1a.at[t, p, d], r1a.at[ch(s, t), d], s1_sem.at[t, p, 0, d], r1_sem.at[ch(s, t), 0, d], to(s, t, 1, d))

    def send_b(s, t, d):
        p = s % 2
        return remote(s1b.at[t, p, d], r1bc.at[ch(s, t), d, 1 - d], s1_sem.at[t, p, 1, d], r1_sem.at[ch(s, t), 1, d], to(s, t, 1, d))

    def send_c(s, t, d):
        p = s % 2
        return remote(s1c.at[t, p, d], r1bc.at[ch(s, t), d, d], s1_sem.at[t, p, 2, d], r1_sem.at[ch(s, t), 1, d], to(s, t, 1, d))

    def send_2a(s, t, d):
        p = s % 2
        return remote(s2a.at[t, p, d], r2a.at[ch(s, t), d], s2_sem.at[t, p, 0, d], r2_sem.at[ch(s, t), 0, d], to(s, t, 2, d))

    def send_2b(s, t, d):
        p = s % 2
        return remote(s2b.at[t, p, d], r2bc.at[ch(s, t), d, 1 - d], s2_sem.at[t, p, 1, d], r2_sem.at[ch(s, t), 1, d], to(s, t, 2, d))

    def send_2c(s, t, d):
        p = s % 2
        return remote(s2c.at[t, p, d], r2bc.at[ch(s, t), d, d], s2_sem.at[t, p, 2, d], r2_sem.at[ch(s, t), 1, d], to(s, t, 2, d))

    def send_x(s, t):
        p = s % 2
        return remote(sx.at[t, p], rx.at[ch(s, t)], x_s.at[t, p], x_r.at[ch(s, t)], xpeer)

    def tile(s, t):
        return pl.ds(pl.multiple_of(ch(s, t) * W + x * COLS, COLS), COLS)

    def send_y(s, t, d):
        here = xg.at[pl.ds(pl.multiple_of(y * SEG, 16), SEG), tile(s, t)]
        return remote(here, here, yg_s.at[t, s % 2, d], yg_r.at[ch(s, t), d], ys[2 * d])

    def relay_y(s, t):
        behind = near(y, 1 - t)
        here = xg.at[pl.ds(pl.multiple_of(behind * SEG, 16), SEG), tile(s, t)]
        return remote(here, here, yg_s.at[t, s % 2, 2], yg_r.at[ch(s, t), 2], ys[2 * t])

    def send_fw(s, t, k):
        here = xg.at[pl.ds(pl.multiple_of(((y + k) % 4) * SEG, 16), SEG), tile(s, t)]
        return remote(here, here, fw_s.at[ch(s, t), k], fw_r.at[ch(s, t), k], xpeer)

    def arrived(ref, sem):
        pltpu.make_async_copy(ref, ref, sem).wait()

    def fetch(s):
        in_load(s).wait()
        in_x(s).wait()

        @pl.when(s + 1 < STEPS)
        def _():
            in_load(s + 1).start()

    def compute(s, ts):
        p = s % 2
        for t in ts:
            b_own = inb[p, :, t * W : (t + 1) * W]
            b_other = inr[:, pl.ds(pl.multiple_of(ch(s, t) * W, W), W)]

            def block(i, _):
                r = pl.ds(pl.multiple_of(i * RZ, 16), RZ)
                v = jnp.dot(ogt[r, 0:TOK], b_own, preferred_element_type=F32)
                v = v + jnp.dot(ogt[r, TOK : 2 * TOK], b_other, preferred_element_type=F32)
                acc[t, p, 0, r, :] = v[:, :COLS]
                acc[t, p, 1, r, :] = v[:, COLS:]
                return 0

            lax.fori_loop(0, NZ, block, 0)

    def send_first(s, ts):
        p = s % 2
        for t in ts:
            m = first(s, t)
            for d in range(2):
                for j in range(4):
                    s1a[t, p, d, j] = acc[t, p, d, rows(s, t, (m + 2) % 4, j), :].astype(BF)
                send_a(s, t, d).start()
            for d in range(2):
                for j in range(4):
                    s1b[t, p, d, j] = acc[t, p, 1 - d, rows(s, t, near(m, d), j), :].astype(BF)
                send_b(s, t, d).start()

    def pass_on(s):
        p = s % 2
        for t in range(2):
            for d in range(2):
                arrived(r1a.at[ch(s, t), d], r1_sem.at[ch(s, t), 0, d])
                for j in range(4):
                    v = acc[t, p, d, rows(s, t, near(first(s, t), d), j), :] + r1a[ch(s, t), d, j].astype(F32)
                    s1c[t, p, d, j] = v.astype(BF)
                send_c(s, t, d).start()

    def sum_first(s):
        p = s % 2
        for t in range(2):
            for d in range(2):
                arrived(r1bc.at[ch(s, t), d], r1_sem.at[ch(s, t), 1, d])
            for h in range(2):
                for j in range(4):
                    v = acc[t, p, h, rows(s, t, first(s, t), j), :]
                    v = v + r1bc[ch(s, t), 0, h, j].astype(F32) + r1bc[ch(s, t), 1, h, j].astype(F32)
                    sums[t, p, h, j] = v
            m = second(s, t)
            for d in range(2):
                s2a[t, p, d] = sums[t, p, d, (m + 2) % 4].astype(BF)
                send_2a(s, t, d).start()
            for d in range(2):
                s2b[t, p, d] = sums[t, p, 1 - d, near(m, d)].astype(BF)
                send_2b(s, t, d).start()
            for d in range(2):
                send_a(s, t, d).wait_send()
                send_b(s, t, d).wait_send()
                send_c(s, t, d).wait_send()

    def pass_on_second(s):
        p = s % 2
        for t in range(2):
            for d in range(2):
                arrived(r2a.at[ch(s, t), d], r2_sem.at[ch(s, t), 0, d])
                v = sums[t, p, d, near(second(s, t), d)] + r2a[ch(s, t), d].astype(F32)
                s2c[t, p, d] = v.astype(BF)
                send_2c(s, t, d).start()

    def sum_second(s):
        p = s % 2
        for t in range(2):
            for d in range(2):
                arrived(r2bc.at[ch(s, t), d], r2_sem.at[ch(s, t), 1, d])
            for h in range(2):
                v = sums[t, p, h, second(s, t)]
                tot[t, p, h] = v + r2bc[ch(s, t), 0, h].astype(F32) + r2bc[ch(s, t), 1, h].astype(F32)
            sx[t, p] = tot[t, p, 1 - x]
            send_x(s, t).start()
            for d in range(2):
                send_2a(s, t, d).wait_send()
                send_2b(s, t, d).wait_send()
                send_2c(s, t, d).wait_send()

    def finish(s):
        p = s % 2
        for t in range(2):
            send_x(s, t).wait()
            v = tot[t, p, x] + rx[ch(s, t)]
            xg[pl.ds(pl.multiple_of(y * SEG, 16), SEG), tile(s, t)] = v.astype(BF)
            for d in range(2):
                send_y(s, t, d).start()
            send_fw(s, t, 0).start()

    def relay_tiles(s):
        for t in range(2):
            for d in range(2):
                send_y(s, t, d).wait()
            relay_y(s, t).start()
            send_fw(s, t, 1).start()
            send_fw(s, t, 3).start()

    def forward(s):
        for t in range(2):
            relay_y(s, t).wait()
            send_fw(s, t, 2).start()

    def complete(s):
        for t in range(2):
            for k in range(4):
                send_fw(s, t, k).wait()

    stages = [
        (2, sum_first),
        (1, pass_on),
        (3, sum_second),
        (4, relay_tiles),
        (0, fetch),
        (0, lambda s: compute(s, (0,))),
        (2, pass_on_second),
        (0, lambda s: send_first(s, (0,))),
        (0, lambda s: compute(s, (1,))),
        (0, lambda s: send_first(s, (1,))),
        (3, finish),
        (6, complete),
        (4, forward),
    ]

    def step(s, _):
        for lag, stage in stages:

            @pl.when(jnp.logical_and(s >= lag, s < STEPS + lag))
            def _(lag=lag, stage=stage):
                stage(s - lag)

        background(s)
        return 0

    lax.fori_loop(0, LAST, step, 0)
    for cp in a_loads:
        cp.wait()

    def send_r(q, d):
        here = rg.at[q, my_rows]
        return remote(here, here, z_s.at[q, d], z_r.at[q, d], zs[2 * d])

    def relay_r(q):
        d = q % 2
        behind = near(z, 1 - d)
        here = rg.at[q, pl.ds(pl.multiple_of(c * HALF + behind * RZ, 16), RZ)]
        return remote(here, here, z_s.at[q, 2], z_r.at[q, 2], zs[2 * d])

    def send_core(q):
        here = rg.at[q, core_rows]
        return remote(here, here, c_s.at[q], c_r.at[q], core)

    def utile(q):
        return pl.ds(pl.multiple_of(((q * 4 + y) * 2 + x) * COLS, COLS), COLS)

    def urows(owner):
        return pl.ds(pl.multiple_of(owner * (OUT // 64), 8), OUT // 64)

    def send_u(q, i):
        k, e = offs[i]
        owner = ((y + k) % 4) * 2 + (x + e) % 2
        return remote(acc.at[q // 2, q % 2, 0, urows(owner)], uo.at[:, utile(q)], u_s.at[q, i], u_r.at[q, i], yx[i])

    for q in range(4):
        v = lax.dot_general(
            xg[...], inr[q * COLS : (q + 1) * COLS, :], (((1,), (1,)), ((), ())), preferred_element_type=F32
        )
        rg[q, my_rows, :] = v.astype(BF)
        for d in range(2):
            send_r(q, d).start()
    own_g.wait()
    for cp in g_sends:
        cp.wait()
    for d in range(2):
        g_pair(d).wait()
    for e in range(2):
        for d in range(2):
            g_far(e, d).start()

    for q in range(5):
        if q < 4:
            for d in range(2):
                send_r(q, d).wait()
            relay_r(q).start()
        if q >= 1:
            relay_r(q - 1).wait()
            send_core(q - 1).start()
    for e in range(2):
        for d in range(2):
            g_far(e, d).wait()
    g_load(0).start()
    for b in range(4):
        if b < 3:
            g_load(b + 1).start()
        g_load(b).wait()
        for i in range(4):
            v = jnp.concatenate([gst[b % 2, i, 0], gst[b % 2, i, 1]], axis=0)
            ogt[b * RZ + i * SEG : b * RZ + (i + 1) * SEG, 0:GK] = v
    for w in range(4):
        send_core(w).wait()
        v = jnp.zeros((RZ, COLS), F32)
        for b in range(4):
            v = v + jnp.dot(
                ogt[b * RZ : (b + 1) * RZ, 0:GK], rg[w, b * GK : (b + 1) * GK, :], preferred_element_type=F32
            )
        acc[w // 2, w % 2, 0, 0:RZ, :] = v
        uo[:, utile(w)] = acc[w // 2, w % 2, 0, urows(y * 2 + x), :]
        for i in range(7):
            send_u(w, i).start()
    for q in range(4):
        for i in range(7):
            send_u(q, i).wait()
    cp = pltpu.make_async_copy(uo, u_out, load_sem.at[0])
    cp.start()
    cp.wait()


def reduce_call(inputs, out_grad, a_inverse, g_inverse):
    anyspace = pl.BlockSpec(memory_space=pl.ANY)
    n = 2 * STEPS
    dma = pltpu.SemaphoreType.DMA
    return pl.pallas_call(
        reduce_kernel,
        out_shape=[
            jax.ShapeDtypeStruct((OUT // 64, IN), F32),
            jax.ShapeDtypeStruct((4, 2, IN // 64, IN), BF),
            jax.ShapeDtypeStruct((4, 2, OUT // 64, OUT), BF),
        ],
        in_specs=[anyspace] * 4,
        out_specs=[anyspace] * 3,
        scratch_shapes=[
            pltpu.VMEM((HALF, 2 * TOK), BF),
            pltpu.VMEM((TOK, HALF), BF),
            pltpu.VMEM((2, TOK, 2 * W), BF),
            pltpu.VMEM((TOK, IN), BF),
            pltpu.VMEM((2, 2, 2, HALF, COLS), F32),
            pltpu.VMEM((2, 2, 2, 4, SEG, COLS), BF),
            pltpu.VMEM((2, 2, 2, 4, SEG, COLS), BF),
            pltpu.VMEM((2, 2, 2, 4, SEG, COLS), BF),
            pltpu.VMEM((n, 2, 4, SEG, COLS), BF),
            pltpu.VMEM((n, 2, 2, 4, SEG, COLS), BF),
            pltpu.VMEM((2, 2, 2, 4, SEG, COLS), F32),
            pltpu.VMEM((2, 2, 2, SEG, COLS), BF),
            pltpu.VMEM((2, 2, 2, SEG, COLS), BF),
            pltpu.VMEM((2, 2, 2, SEG, COLS), BF),
            pltpu.VMEM((n, 2, SEG, COLS), BF),
            pltpu.VMEM((n, 2, 2, SEG, COLS), BF),
            pltpu.VMEM((2, 2, 2, SEG, COLS), F32),
            pltpu.VMEM((2, 2, SEG, COLS), F32),
            pltpu.VMEM((n, SEG, COLS), F32),
            pltpu.VMEM((RZ, IN), BF),
            dma((1,)),
            dma((2,)),
            dma((1 + STEPS,)),
            dma((1 + STEPS,)),
            dma((2, 2, 3, 2)),
            dma((n, 2, 2)),
            dma((2, 2, 3, 2)),
            dma((n, 2, 2)),
            dma((2, 2)),
            dma((n,)),
            dma((2, 2, 3)),
            dma((n, 3)),
            dma((n, 4)),
            dma((n, 4)),
            dma((6,)),
            dma((6,)),
            dma((A_SLICES,)),
            dma((A_SLICES,)),
            dma((2,)),
            dma((2,)),
            dma((2, 2)),
            dma((2, 2)),
            dma((2,)),
            dma((8,)),
            dma((2,)),
            pltpu.VMEM((2, 4, 2, OUT // 64, GK), BF),
            pltpu.VMEM((4, OUT, COLS), BF),
            pltpu.VMEM((OUT // 64, IN), F32),
            dma((4, 3)),
            dma((4, 3)),
            dma((4,)),
            dma((4,)),
            dma((4, 7)),
            dma((4, 7)),
        ],
        compiler_params=pltpu.CompilerParams(
            collective_id=0, has_side_effects=True, vmem_limit_bytes=63 * 1024 * 1024
        ),
        cost_estimate=pl.CostEstimate(flops=29_400_000_000, bytes_accessed=40_000_000, transcendentals=0),
        name="kfac_update",
    )(inputs, out_grad, a_inverse, g_inverse)


def per_device(inputs, out_grad, a_inverse, g_inverse, weights, momentum):
    update = reduce_call(inputs, out_grad, a_inverse, g_inverse)[0]
    new_momentum = 0.9 * momentum + update
    new_weights = weights - 0.5 * new_momentum
    return (new_weights, new_momentum)


def solution(mesh):
    spec = P(("pipe", "dp"), None)
    return jax.shard_map(
        per_device, mesh=mesh, in_specs=(spec,) * 6, out_specs=(spec, spec), check_vma=False
    )
```

time: 280 us -> 207 us (0.74)
  Pallas kernels: 276 us -> 203 us
    pallas_call x2 -> x1, Pallas kernels: 276 us -> 203 us  [reduce_call(): pl.pallas_call(reduce_kernel, out_shape=[jax.ShapeDtypeStruct((OUT // 64,...]
where the time goes in v2:
time: 207 us
  Pallas kernels  203 us (98%)
  other arithmetic  3.67 us (2%)
    pallas_call x1, Pallas kernels, reduce_call(): pl.pallas_call(reduce_kernel, out_shape=[jax.ShapeDtypeStruct((OUT // 64,...  203 us

profile of v2, /device:TPU:0, one launch (start us, length us, event | category | flops | bytes accessed | tf_op | source)
XLA Modules:
  0.0 207.0 jit_solution(17372162150394904360)
XLA Ops:
  0.6 202.7 %kfac_update.1 = (f32[72,4096]{1,0:T(8,128)}, bf16[4,2,64,4096]{3,2,1,0:T(8,128)(2,1)}, bf16[4,2,72,4608]{3,2,1,0:T(8,128)(2,1)}) custom-call(bf16[640,4096]{1,0:T(8,128)(2,1)} %in_ref.1, bf16[640,4608]{1,0:T(8,128)(2,1)} %og_ref.1, bf16[64,4096]{1,0:T(8,128)(2,1)} %a_ref.1, bf16[72,4608]{1,0:T(8,128)(2,1)} %g_ref.1), custom_call_target="tpu_custom_call" | custom-call | flops 29400000512 | bytes 40000000 | tf_op jit(solution)/shard_map/kfac_update/pallas_call | solution.py:488
  203.3 3.7 %multiply_subtract_fusion = (f32[72,4096]{1,0:T(8,128)}, f32[72,4096]{1,0:T(8,128)}) fusion(f32[72,4096]{1,0:T(8,128)} %param.10, f32[72,4096]{1,0:T(8,128)} %get-tuple-element.3, f32[72,4096]{1,0:T(8,128)} %param.11), kind=kLoop, calls=%fused_computation | loop fusion | flops 1179648 | bytes 5898240 | tf_op jit(solution)/shard_map/sub | solution.py:564

commit v3 on v2

v3 whole, which is shorter than its diff:
```python
import functools

import jax
import jax.numpy as jnp
from jax import lax
from jax.experimental import pallas as pl
from jax.experimental.pallas import tpu as pltpu
from jax.sharding import PartitionSpec as P

BF = jnp.bfloat16
F32 = jnp.float32
MESH = pl.DeviceIdType.MESH
NZ, NY = 4, 4
IN, OUT, TOK = 4096, 4608, 640
HALF = OUT // 2
RZ = HALF // NZ
SEG = RZ // NY
W = 256
STEPS = IN // (2 * W)
COLS = 128
ROWHALF = (slice(0, 80), slice(80, 144))
LAST = STEPS + 6
G_PAIR, G_PACK = 11, 13
GK = OUT // 4
SLICE = 512
A_SLICES = IN // SLICE


def coords():
    d = lax.axis_index("dp")
    return d // 16, (d // 4) % 4, (d // 2) % 2, d % 2


def dev(z, y, x, c):
    return {"dp": ((z * 4 + y) * 2 + x) * 2 + c}


def remote(src, dst, ssem, rsem, to):
    return pltpu.make_async_remote_copy(
        src_ref=src, dst_ref=dst, send_sem=ssem, recv_sem=rsem, device_id=to, device_id_type=MESH
    )


def greet(peers):
    barrier = pltpu.get_barrier_semaphore()
    for p in peers:
        pl.semaphore_signal(barrier, inc=1, device_id=p, device_id_type=MESH)
    pl.semaphore_wait(barrier, len(peers))


def reduce_kernel(
    in_ref, og_ref, a_ref, g_ref, u_out, ag_hbm, gg_hbm,
    ogt, ogr, inb, inr, acc, s1, r1a, r1bc,
    sums0, mx, qx, m2, q2a, q2bc, sums, s2, r2a, r2bc, tot, sx, rx, xg,
    load_sem, ld_sem, pair_s, pair_r, s1_sem, r1_sem, s2_sem, r2_sem, x_s, x_r, yg_s, yg_r, fw_s, fw_r, ag_s, ag_r, ra_s, ra_r, gp_s, gp_r, gf_s, gf_r, own_sem,
    al_sem, gl_sem, gst, rg, uo, z_s, z_r, c_s, c_r, u_s, u_r,
):
    z, y, x, c = coords()
    core = dev(z, y, x, 1 - c)
    xpeer = dev(z, y, 1 - x, c)
    zs = [dev((z + k) % 4, y, x, c) for k in (1, 2, 3)]
    ys = [dev(z, (y + k) % 4, x, c) for k in (1, 2, 3)]
    offs = [(k, e) for k in range(4) for e in range(2) if (k, e) != (0, 0)]
    yx = [dev(z, (y + k) % 4, (x + e) % 2, c) for k, e in offs]
    greet([core] + zs + yx)
    my_rows = pl.ds(pl.multiple_of(c * HALF + z * RZ, 16), RZ)
    core_rows = pl.ds(pl.multiple_of(c * HALF, 16), HALF)

    other = pl.multiple_of((1 - c) * HALF, 128)
    mine = pl.multiple_of(c * HALF, 128)

    og_x = remote(og_ref.at[:, pl.ds(other, HALF)], ogr, pair_s.at[0], pair_r.at[0], core)
    og_x.start()

    def in_x(s):
        cols = pl.ds(pl.multiple_of(s * 2 * W, 2 * W), 2 * W)
        return remote(in_ref.at[:, cols], inr.at[:, cols], pair_s.at[1 + s], pair_r.at[1 + s], core)

    in_x(0).start()

    def in_load(s):
        cols = pl.ds(pl.multiple_of(s * 2 * W, 2 * W), 2 * W)
        return pltpu.make_async_copy(in_ref.at[:, cols], inb.at[s % 2], ld_sem.at[s % 2])


    own_a = pltpu.make_async_copy(a_ref, ag_hbm.at[z, c], own_sem.at[0])
    own_g = pltpu.make_async_copy(g_ref, gg_hbm.at[y, x], own_sem.at[1])
    own_a.start()
    own_g.start()
    a_sends = [remote(a_ref, ag_hbm.at[z, c], ag_s.at[k], ag_r.at[k], zs[2 * k]) for k in range(2)]
    g_sends = [remote(g_ref, gg_hbm.at[y, x], ag_s.at[2 + k], ag_r.at[2 + k], ys[2 * k]) for k in range(2)]
    a_fwd = remote(ag_hbm.at[:, c], ag_hbm.at[:, c], ag_s.at[4], ag_r.at[4], core)
    g_own = remote(g_ref, gg_hbm.at[y, x], ag_s.at[5], ag_r.at[5], xpeer)
    for cp in a_sends + g_sends + [g_own]:
        cp.start()

    def relay(out, sem, i, k, other_k, axis, d):
        cols = pl.ds(pl.multiple_of(i * SLICE, SLICE), SLICE)
        from_k = (k + 3) % 4 if d == 0 else (k + 1) % 4
        here = out.at[from_k, other_k, :, cols]
        return remote(here, here, sem[0].at[i], sem[1].at[i], axis[2 * d])

    def relay_a(i, d):
        return relay(ag_hbm, (ra_s, ra_r), i, z, c, zs, d)

    def g_pair(d):
        here = gg_hbm.at[y, 1 - x]
        return remote(here, here, gp_s.at[d], gp_r.at[d], ys[2 * d])

    def g_far(e, d):
        half = OUT // 2
        here = gg_hbm.at[(y + 3 - 2 * d) % 4, e, :, d * half : (d + 1) * half]
        return remote(here, here, gf_s.at[e, d], gf_r.at[e, d], ys[2 * d])

    a_loads = [
        pltpu.make_async_copy(ag_hbm.at[i // 2, i % 2], inr.at[i * 64 : (i + 1) * 64], al_sem.at[i]) for i in range(8)
    ]

    def pack(k):
        there = (y + k) % 4
        cp = pltpu.make_async_copy(gg_hbm.at[there], gst.at[k % 2], gl_sem.at[k % 2])
        cp.start()
        cp.wait()
        for b in range(4):
            cols = slice(b * GK, (b + 1) * GK)
            v = jnp.concatenate([gst[k % 2, 0, :, cols], gst[k % 2, 1, :, cols]], axis=0)
            ogt[pl.ds(pl.multiple_of(b * RZ + there * SEG, 16), SEG), 0:GK] = v

    def between(s, lo, n):
        return jnp.logical_and(s >= lo, s < lo + n)

    def background(s):
        @pl.when(s == 1)
        def _():
            for cp in a_sends:
                cp.wait()

        @pl.when(s == G_PAIR)
        def _():
            g_own.wait()
            for d in range(2):
                g_pair(d).start()

        @pl.when(s == G_PACK)
        def _():
            own_g.wait()
            pack(0)

        @pl.when(between(s, 1, A_SLICES // 2))
        def _():
            relay_a(2 * (s - 1), 0).start()
            relay_a(2 * (s - 1) + 1, 1).start()

        @pl.when(between(s, 3, A_SLICES // 2))
        def _():
            relay_a(2 * (s - 3), 0).wait()
            relay_a(2 * (s - 3) + 1, 1).wait()

        @pl.when(s == 3 + A_SLICES // 2)
        def _():
            own_a.wait()
            a_fwd.start()

        @pl.when(s == 5 + A_SLICES // 2)
        def _():
            a_fwd.wait()
            for cp in a_loads:
                cp.start()

    part = HALF // 6

    def og_load(i):
        return pltpu.make_async_copy(
            og_ref.at[:, pl.ds(mine + i * part, part)], inb.at[i % 2, :, 0:part], ld_sem.at[i % 2]
        )

    og_load(0).start()
    for i in range(6):
        if i < 5:
            og_load(i + 1).start()
        og_load(i).wait()
        for j in range(part // 128):
            ogt[i * part + j * 128 : i * part + (j + 1) * 128, 0:TOK] = inb[i % 2, :, j * 128 : (j + 1) * 128].T
    in_load(0).start()
    og_x.wait()
    in_x(1).start()

    def turn_r(j, _):
        lanes = pl.ds(pl.multiple_of(j * 128, 128), 128)
        ogt[pl.ds(pl.multiple_of(j * 128, 128), 128), TOK : 2 * TOK] = ogr[:, lanes].T
        return 0

    lax.fori_loop(0, HALF // 128, turn_r, 0)

    first, second = (z, y), (y, z)
    stride1, stride2 = (RZ, SEG), (SEG, RZ)
    axis1, axis2 = (zs, ys), (ys, zs)

    def near(k, d):
        return (k + 1) % 4 if d == 0 else (k + 3) % 4

    def rows(t, k, j):
        return pl.ds(pl.multiple_of(k * stride1[t] + j * stride2[t], 16), SEG)

    def ch(s, t):
        return 2 * s + t

    def send_a(s, t, d):
        return remote(s1.at[t, s % 2, d, 0], r1a.at[ch(s, t), d], s1_sem.at[t, s % 2], r1_sem.at[ch(s, t), 0], axis1[t][2 * d])

    def send_bc(s, t, d):
        return remote(s1.at[t, s % 2, d, pl.ds(1, 2)], r1bc.at[ch(s, t), d], s1_sem.at[t, s % 2], r1_sem.at[ch(s, t), 1], axis1[t][2 * d])

    def send_half(s, t, d, h):
        return remote(s1.at[t, s % 2, d, 1 + h], r1bc.at[ch(s, t), d, h], s1_sem.at[t, s % 2], r1_sem.at[ch(s, t), 1], axis1[t][2 * d])

    def send_2a(s, t, d):
        if t == 0:
            half = ROWHALF[d]
            return remote(m2.at[s % 2, d, half], q2a.at[s, half], s2_sem.at[t, s % 2], r2_sem.at[ch(s, t), 0], axis2[t][2 * d])
        return remote(s2.at[s % 2, d, 0], r2a.at[s, d], s2_sem.at[t, s % 2], r2_sem.at[ch(s, t), 0], axis2[t][2 * d])

    def send_2bc(s, t, d):
        if t == 0:
            return remote(m2.at[s % 2, 2 + d], q2bc.at[s, d], s2_sem.at[t, s % 2], r2_sem.at[ch(s, t), 1], axis2[t][2 * d])
        return remote(s2.at[s % 2, d, pl.ds(1, 2)], r2bc.at[s, d], s2_sem.at[t, s % 2], r2_sem.at[ch(s, t), 1], axis2[t][2 * d])

    def far_2(s, t):
        if t == 0:
            return [remote(m2.at[s % 2, 0], q2a.at[s], s2_sem.at[t, s % 2], r2_sem.at[ch(s, t), 0], ys[1])]
        return [
            remote(s2.at[s % 2, d, 0], r2a.at[s, d], s2_sem.at[t, s % 2], r2_sem.at[ch(s, t), 0], zs[1]) for d in range(2)
        ]

    def far_y(s, t):
        here = xg.at[pl.ds(pl.multiple_of(y * SEG, 16), SEG), tile(s, t)]
        return remote(here, here, yg_s.at[t, s % 2], yg_r.at[ch(s, t), 1], ys[1])

    def at_last(s, f, g):
        pl.when(s == STEPS - 1)(f)
        pl.when(s < STEPS - 1)(g)

    def send_x(s, t):
        if t == 0:
            return remote(mx.at[s % 2], qx.at[s], x_s.at[t, s % 2], x_r.at[ch(s, t)], xpeer)
        return remote(sx.at[s % 2], rx.at[s], x_s.at[t, s % 2], x_r.at[ch(s, t)], xpeer)

    def tile(s, t):
        return pl.ds(pl.multiple_of(ch(s, t) * W + x * COLS, COLS), COLS)

    def send_y(s, t, d):
        here = xg.at[pl.ds(pl.multiple_of(y * SEG, 16), SEG), tile(s, t)]
        return remote(here, here, yg_s.at[t, s % 2], yg_r.at[ch(s, t), 0], ys[2 * d])

    def relay_y(s, t):
        behind = near(y, 1 - t)
        here = xg.at[pl.ds(pl.multiple_of(behind * SEG, 16), SEG), tile(s, t)]
        return remote(here, here, yg_s.at[t, s % 2], yg_r.at[ch(s, t), 1], ys[2 * t])

    def send_fw(s, t, k):
        here = xg.at[pl.ds(pl.multiple_of((y // 2 + k) % 2 * (2 * SEG), 16), 2 * SEG), tile(s, t)]
        return remote(here, here, fw_s.at[ch(s, t)], fw_r.at[ch(s, t)], xpeer)

    def arrived(ref, sem):
        pltpu.make_async_copy(ref, ref, sem).wait()

    def fetch(s):
        in_load(s).wait()
        in_x(s).wait()

        @pl.when(s + 1 < STEPS)
        def _():
            in_load(s + 1).start()

        @pl.when(s + 2 < STEPS)
        def _():
            in_x(s + 2).start()

    def compute(s, ts):
        p = s % 2
        for t in ts:
            b_own = inb[p, :, t * W : (t + 1) * W]
            b_other = inr[:, pl.ds(pl.multiple_of(ch(s, t) * W, W), W)]

            def block(i, _):
                r = pl.ds(pl.multiple_of(i * RZ, 16), RZ)
                v = jnp.dot(ogt[r, 0:TOK], b_own, preferred_element_type=F32)
                v = v + jnp.dot(ogt[r, TOK : 2 * TOK], b_other, preferred_element_type=F32)
                acc[t, p, 0, r, :] = v[:, :COLS]
                acc[t, p, 1, r, :] = v[:, COLS:]
                return 0

            lax.fori_loop(0, NZ, block, 0)

    def send_first(s, t):
        p, m = s % 2, first[t]
        for d in range(2):
            for j in range(4):
                s1[t, p, d, 0, j] = acc[t, p, d, rows(t, (m + 2) % 4, j), :].astype(BF)
            send_a(s, t, d).start()
        for d in range(2):
            for j in range(4):
                s1[t, p, d, 2 - d, j] = acc[t, p, 1 - d, rows(t, near(m, d), j), :].astype(BF)

            @pl.when(s == STEPS - 1)
            def _(d=d):
                send_half(s, t, d, 1 - d).start()

    def pass_on(s, t):
        p = s % 2
        arrived(r1a.at[ch(s, t)], r1_sem.at[ch(s, t), 0])
        for d in range(2):
            for j in range(4):
                v = acc[t, p, d, rows(t, near(first[t], d), j), :] + r1a[ch(s, t), d, j].astype(F32)
                s1[t, p, d, 1 + d, j] = v.astype(BF)

            @pl.when(s == STEPS - 1)
            def _(d=d):
                send_half(s, t, d, d).start()

            @pl.when(s < STEPS - 1)
            def _(d=d):
                send_bc(s, t, d).start()

    def sum_first0(s):
        p = s % 2
        arrived(r1bc.at[ch(s, 0)], r1_sem.at[ch(s, 0), 1])

        def summed(h, j):
            v = acc[0, p, h, rows(0, z, j), :]
            return v + r1bc[ch(s, 0), 0, h, j].astype(F32) + r1bc[ch(s, 0), 1, h, j].astype(F32)

        for j in range(4):
            mx[p, j] = summed(1 - x, j).astype(BF)
        send_x(s, 0).start()
        for j in range(4):
            sums0[p, j] = summed(x, j)
        arrived(s1.at[0, p], s1_sem.at[0, p])

    def second0(s):
        p = s % 2
        send_x(s, 0).wait()
        for j in range(4):
            sums0[p, j] = sums0[p, j] + qx[s, j].astype(F32)
        far = sums0[p, (y + 2) % 4].astype(BF)
        for d in range(2):
            m2[p, d] = far

        def direct():
            for d in range(2):
                m2[p, 2 + d] = sums0[p, near(y, d)].astype(BF)
                send_2bc(s, 0, d).start()
            for cp in far_2(s, 0):
                cp.start()

        def relayed():
            for d in range(2):
                send_2a(s, 0, d).start()
            for d in range(2):
                half = ROWHALF[1 - d]
                m2[p, 2 + d, half, :] = sums0[p, near(y, d), half, :].astype(BF)

        at_last(s, direct, relayed)

    def pass_on_second0(s):
        p = s % 2
        arrived(q2a.at[s], r2_sem.at[ch(s, 0), 0])

        @pl.when(s < STEPS - 1)
        def _():
            for d in range(2):
                half = ROWHALF[d]
                v = sums0[p, near(y, d), half, :] + q2a[s, half, :].astype(F32)
                m2[p, 2 + d, half, :] = v.astype(BF)
                send_2bc(s, 0, d).start()

    def finish0(s):
        p = s % 2
        arrived(q2bc.at[s], r2_sem.at[ch(s, 0), 1])
        v = sums0[p, y] + q2bc[s, 0].astype(F32) + q2bc[s, 1].astype(F32)
        v = v + jnp.where(s == STEPS - 1, q2a[s].astype(F32), 0.0)
        xg[pl.ds(pl.multiple_of(y * SEG, 16), SEG), tile(s, 0)] = v.astype(BF)
        for d in range(2):
            send_y(s, 0, d).start()
        pl.when(s == STEPS - 1)(lambda: far_y(s, 0).start())
        arrived(m2.at[p, pl.ds(1, 3)], s2_sem.at[0, p])

    def sum_first1(s):
        t, p, m = 1, s % 2, z
        arrived(r1bc.at[ch(s, t)], r1_sem.at[ch(s, t), 1])
        for h in range(2):
            for j in range(4):
                v = acc[t, p, h, rows(t, y, j), :]
                sums[p, h, j] = v + r1bc[ch(s, t), 0, h, j].astype(F32) + r1bc[ch(s, t), 1, h, j].astype(F32)
        for d in range(2):
            s2[p, d, 0] = sums[p, d, (m + 2) % 4].astype(BF)
        for d in range(2):
            s2[p, d, 2 - d] = sums[p, 1 - d, near(m, d)].astype(BF)

        def direct():
            for d in range(2):
                s2[p, d, 1 + d] = sums[p, d, near(m, d)].astype(BF)
                send_2bc(s, t, d).start()
            for cp in far_2(s, t):
                cp.start()

        def relayed():
            for d in range(2):
                send_2a(s, t, d).start()

        at_last(s, direct, relayed)
        arrived(s1.at[t, p], s1_sem.at[t, p])

    def pass_on_second1(s):
        p = s % 2
        arrived(r2a.at[s], r2_sem.at[ch(s, 1), 0])

        @pl.when(s < STEPS - 1)
        def _():
            for d in range(2):
                v = sums[p, d, near(z, d)] + r2a[s, d].astype(F32)
                s2[p, d, 1 + d] = v.astype(BF)
                send_2bc(s, 1, d).start()

    def sum_second1(s):
        p = s % 2
        arrived(r2bc.at[s], r2_sem.at[ch(s, 1), 1])
        for h in range(2):
            v = sums[p, h, z] + r2bc[s, 0, h].astype(F32) + r2bc[s, 1, h].astype(F32)
            tot[p, h] = v + jnp.where(s == STEPS - 1, r2a[s, h].astype(F32), 0.0)
        sx[p] = tot[p, 1 - x]
        send_x(s, 1).start()
        arrived(s2.at[p], s2_sem.at[1, p])

    def finish1(s):
        send_x(s, 1).wait()
        v = tot[s % 2, x] + rx[s]
        xg[pl.ds(pl.multiple_of(y * SEG, 16), SEG), tile(s, 1)] = v.astype(BF)
        for d in range(2):
            send_y(s, 1, d).start()
        pl.when(s == STEPS - 1)(lambda: far_y(s, 1).start())

    def relay_tiles(s, t):
        arrived(xg.at[pl.ds(0, 2 * SEG), tile(s, t)], yg_r.at[ch(s, t), 0])
        pl.when(s < STEPS - 1)(lambda: relay_y(s, t).start())
        send_fw(s, t, 0).start()

    def forward(s, t):
        arrived(xg.at[pl.ds(0, SEG), tile(s, t)], yg_r.at[ch(s, t), 1])
        send_fw(s, t, 1).start()
        arrived(xg.at[pl.ds(0, 3 * SEG), tile(s, t)], yg_s.at[t, s % 2])

    def complete(s, t):
        whole = xg.at[:, tile(s, t)]
        arrived(whole, fw_s.at[ch(s, t)])
        arrived(whole, fw_r.at[ch(s, t)])

    def both(f):
        def g(s):
            for t in range(2):
                f(s, t)

        return g

    stages = [
        (2, sum_first0),
        (2, sum_first1),
        (1, both(pass_on)),
        (3, pass_on_second0),
        (3, sum_second1),
        (4, both(relay_tiles)),
        (0, fetch),
        (0, lambda s: compute(s, (0,))),
        (2, pass_on_second1),
        (0, lambda s: send_first(s, 0)),
        (0, lambda s: compute(s, (1,))),
        (0, lambda s: send_first(s, 1)),
        (3, finish0),
        (2, second0),
        (3, finish1),
        (6, both(complete)),
        (4, both(forward)),
    ]

    def step(s, _):
        for lag, stage in stages:

            @pl.when(jnp.logical_and(s >= lag, s < STEPS + lag))
            def _(lag=lag, stage=stage):
                stage(s - lag)

        background(s)
        return 0

    lax.fori_loop(0, LAST, step, 0)
    for cp in a_loads:
        cp.wait()

    def send_r(q, d):
        here = rg.at[q, my_rows]
        return remote(here, here, z_s.at[q, d], z_r.at[q, d], zs[2 * d])

    def relay_r(q):
        d = q % 2
        behind = near(z, 1 - d)
        here = rg.at[q, pl.ds(pl.multiple_of(c * HALF + behind * RZ, 16), RZ)]
        return remote(here, here, z_s.at[q, 2], z_r.at[q, 2], zs[2 * d])

    def send_core(q):
        here = rg.at[q, core_rows]
        return remote(here, here, c_s.at[q], c_r.at[q], core)

    def utile(q):
        return pl.ds(pl.multiple_of(((q * 4 + y) * 2 + x) * COLS, COLS), COLS)

    def urows(owner):
        return pl.ds(pl.multiple_of(owner * (OUT // 64), 8), OUT // 64)

    def send_u(q, i):
        k, e = offs[i]
        owner = ((y + k) % 4) * 2 + (x + e) % 2
        return remote(acc.at[q // 2, q % 2, 0, urows(owner)], uo.at[:, utile(q)], u_s.at[q, i], u_r.at[q, i], yx[i])

    def right(q):
        v = lax.dot_general(
            xg[...], inr[q * COLS : (q + 1) * COLS, :], (((1,), (1,)), ((), ())), preferred_element_type=F32
        )
        rg[q, my_rows, :] = v.astype(BF)
        for d in range(2):
            send_r(q, d).start()

    def pass_right(q):
        for d in range(2):
            send_r(q, d).wait()
        relay_r(q).start()

    def share_right(q):
        relay_r(q).wait()
        send_core(q).start()

    def update(q):
        send_core(q).wait()
        v = jnp.zeros((RZ, COLS), F32)
        for b in range(4):
            v = v + jnp.dot(
                ogt[b * RZ : (b + 1) * RZ, 0:GK], rg[q, b * GK : (b + 1) * GK, :], preferred_element_type=F32
            )
        acc[q // 2, q % 2, 0, 0:RZ, :] = v
        uo[:, utile(q)] = acc[q // 2, q % 2, 0, urows(y * 2 + x), :]
        for i in range(7):
            send_u(q, i).start()

    right(0)
    right(1)
    for cp in g_sends:
        cp.wait()
    for d in range(2):
        g_pair(d).wait()
    for e in range(2):
        for d in range(2):
            g_far(e, d).start()
    pass_right(0)
    right(2)
    pass_right(1)
    pack(1)
    right(3)
    share_right(0)
    pass_right(2)
    pack(3)
    share_right(1)
    pass_right(3)
    for e in range(2):
        for d in range(2):
            g_far(e, d).wait()
    pack(2)
    update(0)
    share_right(2)
    update(1)
    share_right(3)
    update(2)
    update(3)
    for q in range(4):
        for i in range(7):
            send_u(q, i).wait()
    cp = pltpu.make_async_copy(uo, u_out, load_sem.at[0])
    cp.start()
    cp.wait()


def reduce_call(inputs, out_grad, a_inverse, g_inverse):
    anyspace = pl.BlockSpec(memory_space=pl.ANY)
    n = 2 * STEPS
    dma = pltpu.SemaphoreType.DMA
    return pl.pallas_call(
        reduce_kernel,
        out_shape=[
            jax.ShapeDtypeStruct((OUT // 64, IN), F32),
            jax.ShapeDtypeStruct((4, 2, IN // 64, IN), BF),
            jax.ShapeDtypeStruct((4, 2, OUT // 64, OUT), BF),
        ],
        in_specs=[anyspace] * 4,
        out_specs=[anyspace] * 3,
        scratch_shapes=[
            pltpu.VMEM((HALF, 2 * TOK), BF),
            pltpu.VMEM((TOK, HALF), BF),
            pltpu.VMEM((2, TOK, 2 * W), BF),
            pltpu.VMEM((TOK, IN), BF),
            pltpu.VMEM((2, 2, 2, HALF, COLS), F32),
            pltpu.VMEM((2, 2, 2, 3, 4, SEG, COLS), BF),
            pltpu.VMEM((n, 2, 4, SEG, COLS), BF),
            pltpu.VMEM((n, 2, 2, 4, SEG, COLS), BF),
            pltpu.VMEM((2, 4, SEG, COLS), F32),
            pltpu.VMEM((2, 4, SEG, COLS), BF),
            pltpu.VMEM((STEPS, 4, SEG, COLS), BF),
            pltpu.VMEM((2, 4, SEG, COLS), BF),
            pltpu.VMEM((STEPS, SEG, COLS), BF),
            pltpu.VMEM((STEPS, 2, SEG, COLS), BF),
            pltpu.VMEM((2, 2, 4, SEG, COLS), F32),
            pltpu.VMEM((2, 2, 3, SEG, COLS), BF),
            pltpu.VMEM((STEPS, 2, SEG, COLS), BF),
            pltpu.VMEM((STEPS, 2, 2, SEG, COLS), BF),
            pltpu.VMEM((2, 2, SEG, COLS), F32),
            pltpu.VMEM((2, SEG, COLS), F32),
            pltpu.VMEM((STEPS, SEG, COLS), F32),
            pltpu.VMEM((RZ, IN), BF),
            dma((1,)),
            dma((2,)),
            dma((1 + STEPS,)),
            dma((1 + STEPS,)),
            dma((2, 2)),
            dma((n, 2)),
            dma((2, 2)),
            dma((n, 2)),
            dma((2, 2)),
            dma((n,)),
            dma((2, 2)),
            dma((n, 2)),
            dma((n,)),
            dma((n,)),
            dma((6,)),
            dma((6,)),
            dma((A_SLICES,)),
            dma((A_SLICES,)),
            dma((2,)),
            dma((2,)),
            dma((2, 2)),
            dma((2, 2)),
            dma((2,)),
            dma((8,)),
            dma((2,)),
            pltpu.VMEM((2, 2, OUT // 64, OUT), BF),
            pltpu.VMEM((4, OUT, COLS), BF),
            pltpu.VMEM((OUT // 64, IN), F32),
            dma((4, 3)),
            dma((4, 3)),
            dma((4,)),
            dma((4,)),
            dma((4, 7)),
            dma((4, 7)),
        ],
        compiler_params=pltpu.CompilerParams(
            collective_id=0, has_side_effects=True, vmem_limit_bytes=63 * 1024 * 1024
        ),
        cost_estimate=pl.CostEstimate(flops=29_400_000_000, bytes_accessed=40_000_000, transcendentals=0),
        name="kfac_update",
    )(inputs, out_grad, a_inverse, g_inverse)


def per_device(inputs, out_grad, a_inverse, g_inverse, weights, momentum):
    update = reduce_call(inputs, out_grad, a_inverse, g_inverse)[0]
    new_momentum = 0.9 * momentum + update
    new_weights = weights - 0.5 * new_momentum
    return (new_weights, new_momentum)


def solution(mesh):
    spec = P(("pipe", "dp"), None)
    return jax.shard_map(
        per_device, mesh=mesh, in_specs=(spec,) * 6, out_specs=(spec, spec), check_vma=False
    )
```

time: 207 us -> 204 us (0.986)
  Pallas kernels: 203 us -> 199 us
    pallas_call x1, Pallas kernels: 203 us -> 199 us  [reduce_call(): pl.pallas_call(reduce_kernel, out_shape=[jax.ShapeDtypeStruct((OUT // 64,...]
where the time goes in v3:
time: 204 us; the launch traced here: 203 us
  Pallas kernels  199 us (98%)
  other arithmetic  3.67 us (2%)
    pallas_call x1, Pallas kernels, reduce_call(): pl.pallas_call(reduce_kernel, out_shape=[jax.ShapeDtypeStruct((OUT // 64,...  199 us

profile of v3, /device:TPU:0, one launch (start us, length us, event | category | flops | bytes accessed | tf_op | source)
XLA Modules:
  0.0 203.3 jit_solution(13157194220219574234)
XLA Ops:
  0.6 199.0 %kfac_update.1 = (f32[72,4096]{1,0:T(8,128)}, bf16[4,2,64,4096]{3,2,1,0:T(8,128)(2,1)}, bf16[4,2,72,4608]{3,2,1,0:T(8,128)(2,1)}) custom-call(bf16[640,4096]{1,0:T(8,128)(2,1)} %in_ref.1, bf16[640,4608]{1,0:T(8,128)(2,1)} %og_ref.1, bf16[64,4096]{1,0:T(8,128)(2,1)} %a_ref.1, bf16[72,4608]{1,0:T(8,128)(2,1)} %g_ref.1), custom_call_target="tpu_custom_call" | custom-call | flops 29400000512 | bytes 40000000 | tf_op jit(solution)/shard_map/kfac_update/pallas_call | solution.py:594
  199.7 3.7 %multiply_subtract_fusion = (f32[72,4096]{1,0:T(8,128)}, f32[72,4096]{1,0:T(8,128)}) fusion(f32[72,4096]{1,0:T(8,128)} %param.10, f32[72,4096]{1,0:T(8,128)} %get-tuple-element.3, f32[72,4096]{1,0:T(8,128)} %param.11), kind=kLoop, calls=%fused_computation | loop fusion | flops 1179648 | bytes 5898240 | tf_op jit(solution)/shard_map/sub | solution.py:672

commit v4 on v3

--- a/solution.py
+++ b/solution.py
@@ -20,7 +20,7 @@
 COLS = 128
 ROWHALF = (slice(0, 80), slice(80, 144))
 LAST = STEPS + 6
-G_PAIR, G_PACK = 11, 13
+G_PAIR, G_PACK = 11, 12
 GK = OUT // 4
 SLICE = 512
 A_SLICES = IN // SLICE
@@ -52,8 +52,8 @@
     in_ref, og_ref, a_ref, g_ref, u_out, ag_hbm, gg_hbm,
     ogt, ogr, inb, inr, acc, s1, r1a, r1bc,
     sums0, mx, qx, m2, q2a, q2bc, sums, s2, r2a, r2bc, tot, sx, rx, xg,
-    load_sem, ld_sem, pair_s, pair_r, s1_sem, r1_sem, s2_sem, r2_sem, x_s, x_r, yg_s, yg_r, fw_s, fw_r, ag_s, ag_r, ra_s, ra_r, gp_s, gp_r, gf_s, gf_r, own_sem,
-    al_sem, gl_sem, gst, rg, uo, z_s, z_r, c_s, c_r, u_s, u_r,
+    ld_sem, pair_s, pair_r, s1_sem, r1_sem, s2_sem, r2_sem, x_s, x_r, yg_s, yg_r, fw_s, fw_r, ag_s, ag_r, ra_s, ra_r, gp_s, gp_r, gf_s, gf_r, own_sem,
+    al_sem, gl_sem, st_sem, gst, rg, uo, z_s, z_r, c_s, c_r, u_s, u_r,
 ):
     z, y, x, c = coords()
     core = dev(z, y, x, 1 - c)
@@ -65,6 +65,7 @@
     greet([core] + zs + yx)
     my_rows = pl.ds(pl.multiple_of(c * HALF + z * RZ, 16), RZ)
     core_rows = pl.ds(pl.multiple_of(c * HALF, 16), HALF)
+    other_rows = pl.ds(pl.multiple_of((1 - c) * HALF, 16), HALF)
 
     other = pl.multiple_of((1 - c) * HALF, 128)
     mine = pl.multiple_of(c * HALF, 128)
@@ -506,8 +507,8 @@
         here = rg.at[q, pl.ds(pl.multiple_of(c * HALF + behind * RZ, 16), RZ)]
         return remote(here, here, z_s.at[q, 2], z_r.at[q, 2], zs[2 * d])
 
-    def send_core(q):
-        here = rg.at[q, core_rows]
+    def send_core(q, k):
+        here = rg.at[q, pl.ds(pl.multiple_of(c * HALF + ((z + k) % 4) * RZ, 16), RZ)]
         return remote(here, here, c_s.at[q], c_r.at[q], core)
 
     def utile(q):
@@ -528,18 +529,22 @@
         rg[q, my_rows, :] = v.astype(BF)
         for d in range(2):
             send_r(q, d).start()
+        send_core(q, 0).start()
 
     def pass_right(q):
         for d in range(2):
             send_r(q, d).wait()
         relay_r(q).start()
+        send_core(q, 1).start()
+        send_core(q, 3).start()
 
     def share_right(q):
         relay_r(q).wait()
-        send_core(q).start()
+        send_core(q, 2).start()
 
     def update(q):
-        send_core(q).wait()
+        arrived(rg.at[q, core_rows], c_s.at[q])
+        arrived(rg.at[q, other_rows], c_r.at[q])
         v = jnp.zeros((RZ, COLS), F32)
         for b in range(4):
             v = v + jnp.dot(
@@ -579,12 +584,16 @@
     share_right(3)
     update(2)
     update(3)
+    def store(q):
+        cols = pl.ds(q * 8 * COLS, 8 * COLS)
+        return pltpu.make_async_copy(uo.at[:, cols], u_out.at[:, cols], st_sem.at[q])
+
     for q in range(4):
         for i in range(7):
             send_u(q, i).wait()
-    cp = pltpu.make_async_copy(uo, u_out, load_sem.at[0])
-    cp.start()
-    cp.wait()
+        store(q).start()
+    for q in range(4):
+        store(q).wait()
 
 
 def reduce_call(inputs, out_grad, a_inverse, g_inverse):
@@ -623,7 +632,6 @@
             pltpu.VMEM((2, SEG, COLS), F32),
             pltpu.VMEM((STEPS, SEG, COLS), F32),
             pltpu.VMEM((RZ, IN), BF),
-            dma((1,)),
             dma((2,)),
             dma((1 + STEPS,)),
             dma((1 + STEPS,)),
@@ -648,6 +656,7 @@
             dma((2,)),
             dma((8,)),
             dma((2,)),
+            dma((4,)),
             pltpu.VMEM((2, 2, OUT // 64, OUT), BF),
             pltpu.VMEM((4, OUT, COLS), BF),
             pltpu.VMEM((OUT // 64, IN), F32),

time: 204 us -> 202 us (level)
  no operation moved by 1% of the time
where the time goes in v4:
time: 202 us
  Pallas kernels  197 us (98%)
  other arithmetic  3.67 us (2%)
    pallas_call x1, Pallas kernels, reduce_call(): pl.pallas_call(reduce_kernel, out_shape=[jax.ShapeDtypeStruct((OUT // 64,...  197 us

profile of v4, /device:TPU:0, one launch (start us, length us, event | category | flops | bytes accessed | tf_op | source)
XLA Modules:
  0.0 201.6 jit_solution(7127804506748345553)
XLA Ops:
  0.6 197.3 %kfac_update.1 = (f32[72,4096]{1,0:T(8,128)}, bf16[4,2,64,4096]{3,2,1,0:T(8,128)(2,1)}, bf16[4,2,72,4608]{3,2,1,0:T(8,128)(2,1)}) custom-call(bf16[640,4096]{1,0:T(8,128)(2,1)} %in_ref.1, bf16[640,4608]{1,0:T(8,128)(2,1)} %og_ref.1, bf16[64,4096]{1,0:T(8,128)(2,1)} %a_ref.1, bf16[72,4608]{1,0:T(8,128)(2,1)} %g_ref.1), custom_call_target="tpu_custom_call" | custom-call | flops 29400000512 | bytes 40000000 | tf_op jit(solution)/shard_map/kfac_update/pallas_call | solution.py:603
  197.9 3.7 %multiply_subtract_fusion = (f32[72,4096]{1,0:T(8,128)}, f32[72,4096]{1,0:T(8,128)}) fusion(f32[72,4096]{1,0:T(8,128)} %param.10, f32[72,4096]{1,0:T(8,128)} %get-tuple-element.3, f32[72,4096]{1,0:T(8,128)} %param.11), kind=kLoop, calls=%fused_computation | loop fusion | flops 1179648 | bytes 5898240 | tf_op jit(solution)/shard_map/sub | solution.py:681

commit v5 on v4

--- a/solution.py
+++ b/solution.py
@@ -259,7 +259,7 @@
         return remote(here, here, yg_s.at[t, s % 2], yg_r.at[ch(s, t), 1], ys[2 * t])
 
     def send_fw(s, t, k):
-        here = xg.at[pl.ds(pl.multiple_of((y // 2 + k) % 2 * (2 * SEG), 16), 2 * SEG), tile(s, t)]
+        here = xg.at[pl.ds(pl.multiple_of((y + k) % 4 * SEG, 16), SEG), tile(s, t)]
         return remote(here, here, fw_s.at[ch(s, t)], fw_r.at[ch(s, t)], xpeer)
 
     def arrived(ref, sem):
@@ -383,6 +383,7 @@
         xg[pl.ds(pl.multiple_of(y * SEG, 16), SEG), tile(s, 0)] = v.astype(BF)
         for d in range(2):
             send_y(s, 0, d).start()
+        send_fw(s, 0, 0).start()
         pl.when(s == STEPS - 1)(lambda: far_y(s, 0).start())
         arrived(m2.at[p, pl.ds(1, 3)], s2_sem.at[0, p])
 
@@ -439,16 +440,18 @@
         xg[pl.ds(pl.multiple_of(y * SEG, 16), SEG), tile(s, 1)] = v.astype(BF)
         for d in range(2):
             send_y(s, 1, d).start()
+        send_fw(s, 1, 0).start()
         pl.when(s == STEPS - 1)(lambda: far_y(s, 1).start())
 
     def relay_tiles(s, t):
         arrived(xg.at[pl.ds(0, 2 * SEG), tile(s, t)], yg_r.at[ch(s, t), 0])
         pl.when(s < STEPS - 1)(lambda: relay_y(s, t).start())
-        send_fw(s, t, 0).start()
+        send_fw(s, t, 1).start()
+        send_fw(s, t, 3).start()
 
     def forward(s, t):
         arrived(xg.at[pl.ds(0, SEG), tile(s, t)], yg_r.at[ch(s, t), 1])
-        send_fw(s, t, 1).start()
+        send_fw(s, t, 2).start()
         arrived(xg.at[pl.ds(0, 3 * SEG), tile(s, t)], yg_s.at[t, s % 2])
 
     def complete(s, t):
@@ -476,9 +479,9 @@
         (0, lambda s: send_first(s, 0)),
         (0, lambda s: compute(s, (1,))),
         (0, lambda s: send_first(s, 1)),
-        (3, finish0),
         (2, second0),
         (3, finish1),
+        (3, finish0),
         (6, both(complete)),
         (4, both(forward)),
     ]

time: 202 us -> 203 us (level)
  no operation moved by 1% of the time
where the time goes in v5:
time: 203 us
  Pallas kernels  199 us (98%)
  other arithmetic  3.67 us (2%)
    pallas_call x1, Pallas kernels, reduce_call(): pl.pallas_call(reduce_kernel, out_shape=[jax.ShapeDtypeStruct((OUT // 64,...  199 us

profile of v5, /device:TPU:0, one launch (start us, length us, event | category | flops | bytes accessed | tf_op | source)
XLA Modules:
  0.0 203.1 jit_solution(10258673285936354608)
XLA Ops:
  0.6 198.8 %kfac_update.1 = (f32[72,4096]{1,0:T(8,128)}, bf16[4,2,64,4096]{3,2,1,0:T(8,128)(2,1)}, bf16[4,2,72,4608]{3,2,1,0:T(8,128)(2,1)}) custom-call(bf16[640,4096]{1,0:T(8,128)(2,1)} %in_ref.1, bf16[640,4608]{1,0:T(8,128)(2,1)} %og_ref.1, bf16[64,4096]{1,0:T(8,128)(2,1)} %a_ref.1, bf16[72,4608]{1,0:T(8,128)(2,1)} %g_ref.1), custom_call_target="tpu_custom_call" | custom-call | flops 29400000512 | bytes 40000000 | tf_op jit(solution)/shard_map/kfac_update/pallas_call | solution.py:606
  199.4 3.7 %multiply_subtract_fusion = (f32[72,4096]{1,0:T(8,128)}, f32[72,4096]{1,0:T(8,128)}) fusion(f32[72,4096]{1,0:T(8,128)} %param.10, f32[72,4096]{1,0:T(8,128)} %get-tuple-element.3, f32[72,4096]{1,0:T(8,128)} %param.11), kind=kLoop, calls=%fused_computation | loop fusion | flops 1179648 | bytes 5898240 | tf_op jit(solution)/shard_map/sub | solution.py:684
